TPU v7x, 256 devices: a whole 4x4x8 slice. The times are simulated.
256 devices in a mesh: seq: 64 (over x, z_lo, y), rep: 4 (over z_hi, core).
Axes of the slice: x: 4, y: 4, z: 8 (z_hi: 2, z_lo: 4; z = z_hi * 4 + z_lo), core: 2. Of those that a mesh axis runs over, the one named last changes fastest.
Arguments:
- query: bfloat16 [65536, 1024], P('seq', 'rep'), parts along dimension 1
- keys: bfloat16 [65536, 1024], P('seq', 'rep'), parts along dimension 1
- values: bfloat16 [65536, 1024], P('seq', 'rep'), parts along dimension 1, may hold values from -6 to 6
- grad_out: bfloat16 [65536, 1024], P('seq', 'rep'), parts along dimension 1, may hold values from -48 to 48
- offsets: int32 [3, 8], P(None, 'rep'), parts along dimension 1, may hold values from 0 to 127, as said below
Outputs:
- attended: float32 [65536, 1024], P('seq', 'rep'), parts along dimension 1
- grad_query: float32 [65536, 1024], P('seq', 'rep'), parts along dimension 1
- grad_keys: float32 [65536, 1024], P('seq', 'rep'), parts along dimension 1
- grad_values: float32 [65536, 1024], P('seq', 'rep'), parts along dimension 1
There are 4 independent parts, one for each index of `rep`. A program takes and returns all parts, laid end to end along the dimension named above; each array names one. Nothing has to cross between parts.
Inputs may be any that keep to these rules, and one draw needn't show every extreme that they name: offsets[l, h] lies in 0 to r - 1 for the dilation r of level l + 1 (8, 32, 128); at level 3 some head has offset 128 - 1, and at level 1 some head has offset 0.
All inputs are finite; a program needn't handle non-finite values.
Results may differ from a plain program's by a relative error of at most 0.0062.
The roundings to bfloat16 on the way count: a program that leaves them out, or rounds other values in their place, can miss the bound.
Values may be sent and summed in bfloat16 or wider, within the bound.
A program may use at most 128 MiB of HBM per device.

v0:
```python
from functools import reduce

import jax
import jax.numpy as jnp
from jax import lax
from jax.sharding import PartitionSpec as P

HEADS = 2
KEYS = 512


def partner_2(block, axis, stride):
    count = lax.axis_size(axis)
    route = []
    for low in range(count):
        high = low | 1 << stride
        if high != low and high < count:
            route += [(low, high), (high, low)]
    return lax.ppermute(block, axis, route)


def dilate(source, dilation, offsets_row):
    row_count = source.shape[0] // dilation
    folded = source.reshape((row_count, dilation) + source.shape[1:])
    columns = [
        lax.dynamic_index_in_dim(folded[:, :, head], offsets_row[head], 1, keepdims=False)
        for head in range(source.shape[1])
    ]
    return jnp.stack(columns, 1)


def spread(dilated, dilation, offsets_row):
    row_count, head_count = (dilated.shape[0], dilated.shape[1])
    selector = (jnp.arange(dilation, dtype=jnp.int32)[:, None] == offsets_row[None, :]).astype(
        dilated.dtype
    )
    selector = selector.reshape((1, dilation, head_count) + (1,) * (dilated.ndim - 2))
    return (dilated[:, None] * selector).reshape((row_count * dilation,) + dilated.shape[1:])


def spread_max(row_max, dilation, offsets_row):
    row_count, head_count = row_max.shape
    member_mask = jnp.arange(dilation, dtype=jnp.int32)[:, None] == offsets_row[None, :]
    member_mask = jnp.broadcast_to(member_mask[None], (row_count, dilation, head_count)).reshape(
        row_count * dilation, head_count
    )
    broad = jnp.broadcast_to(row_max[:, None], (row_count, dilation, head_count)).reshape(
        row_count * dilation, head_count
    )
    return jnp.where(member_mask, broad, -jnp.inf)


def attend(query_rows, key_rows, value_rows, factor):
    scores = (
        jnp.einsum("qhd,khd->hqk", query_rows, key_rows, preferred_element_type=jnp.float32)
        * factor
    )
    row_max = jnp.max(scores, -1)
    powers = jnp.exp(scores - row_max[..., None])
    total = jnp.sum(powers, -1)
    weights = powers.astype(jnp.bfloat16)
    weighted = jnp.einsum("hqk,khd->qhd", weights, value_rows, preferred_element_type=jnp.float32)
    return (row_max.T, total.T, weighted)


def gradients(query_rows, key_rows, value_rows, dout_rows, log_rows, delta_rows, factor):
    scores = (
        jnp.einsum("qhd,khd->hqk", query_rows, key_rows, preferred_element_type=jnp.float32)
        * factor
    )
    probs = jnp.exp(scores - log_rows.T[:, :, None])
    grad_probs = jnp.einsum(
        "qhd,khd->hqk", dout_rows, value_rows, preferred_element_type=jnp.float32
    )
    grad_scores = probs * (grad_probs - delta_rows.T[:, :, None])
    grad_low = grad_scores.astype(jnp.bfloat16)
    results = []
    results.append(
        factor * jnp.einsum("hqk,khd->qhd", grad_low, key_rows, preferred_element_type=jnp.float32)
    )
    results.append(
        factor
        * jnp.einsum("hqk,qhd->khd", grad_low, query_rows, preferred_element_type=jnp.float32)
    )
    results.append(
        jnp.einsum(
            "hqk,qhd->khd",
            probs.astype(jnp.bfloat16),
            dout_rows,
            preferred_element_type=jnp.float32,
        )
    )
    return tuple(results)


def combine_pair(which_bit, position, own_part, partner):
    is_lower = position // 2**which_bit % 2 == 0
    return jnp.where(
        is_lower, jnp.concatenate([own_part, partner], 1), jnp.concatenate([partner, own_part], 1)
    )


def spread_keys(stacked, level_bits, position):
    for which_bit in range(level_bits):
        partner = partner_2(stacked, "seq", which_bit)
        stacked = combine_pair(which_bit, position, stacked, partner)
    return stacked


def fold_grads(stacked, level_bits, position):
    for which_bit in reversed(range(level_bits)):
        half_rows = stacked.shape[1] // 2
        is_lower = position // 2**which_bit % 2 == 0
        low_part = stacked[:, :half_rows]
        high_part = stacked[:, half_rows:]
        outgoing = jnp.where(is_lower, high_part, low_part)
        retained = jnp.where(is_lower, low_part, high_part)
        stacked = retained + partner_2(outgoing.astype(jnp.bfloat16), "seq", which_bit).astype(
            outgoing.dtype
        )
    return stacked


def body(query, keys, values, grad_out, offsets):
    tok_rows, feature_width = query.shape
    head_dim = feature_width // HEADS
    factor = head_dim ** (-0.5)
    seq_devices = lax.axis_size("seq")
    position = lax.axis_index("seq")
    shape3 = (tok_rows, HEADS, head_dim)
    query3 = query.reshape(shape3)
    keys3 = keys.reshape(shape3)
    values3 = values.reshape(shape3)
    dout3 = grad_out.reshape(shape3)

    def segments(source):
        return source.reshape((-1, KEYS) + source.shape[1:])

    first = lax.map(
        lambda blocks: attend(blocks[0], blocks[1], blocks[2], factor),
        (segments(query3), segments(keys3), segments(values3)),
    )
    maxima = [first[0].reshape(tok_rows, HEADS)]
    totals = [first[1].reshape(tok_rows, HEADS)]
    weighted_list = [first[2].reshape(shape3)]
    plans = []
    for level in range(3):
        level_span = (4, min(16, seq_devices), seq_devices)[level]
        dilation = level_span * tok_rows // KEYS
        level_bits = level_span.bit_length() - 1
        offsets_row = offsets[level]
        query_rows = dilate(query3, dilation, offsets_row)
        own_keys = jnp.stack(
            (dilate(keys3, dilation, offsets_row), dilate(values3, dilation, offsets_row))
        )
        if level_span == seq_devices:
            key_value = lax.all_gather(own_keys, "seq", axis=1, tiled=True)
        else:
            key_value = spread_keys(own_keys, level_bits, position)
        row_max, total, weighted = attend(query_rows, key_value[0], key_value[1], factor)
        maxima.append(spread_max(row_max, dilation, offsets_row))
        totals.append(spread(total, dilation, offsets_row))
        weighted_list.append(spread(weighted, dilation, offsets_row))
        plans.append(
            (level_span, dilation, level_bits, offsets_row, query_rows, own_keys, key_value)
        )
    peak = reduce(jnp.maximum, maxima)
    factors = [jnp.exp(item - peak) for item in maxima]
    denominator = factors[0] * totals[0]
    numerator = factors[0][..., None] * weighted_list[0]
    for level in range(1, 4):
        denominator = denominator + factors[level] * totals[level]
        numerator = numerator + factors[level][..., None] * weighted_list[level]
    attended = numerator / denominator[..., None]
    log_total = peak + jnp.log(denominator)
    delta = jnp.sum(dout3.astype(jnp.float32) * attended, -1)
    local = lax.map(
        lambda blocks: gradients(
            blocks[0], blocks[1], blocks[2], blocks[3], blocks[4], blocks[5], factor
        ),
        (
            segments(query3),
            segments(keys3),
            segments(values3),
            segments(dout3),
            segments(log_total),
            segments(delta),
        ),
    )
    grad_q = local[0].reshape(shape3)
    grad_k = local[1].reshape(shape3)
    grad_v = local[2].reshape(shape3)
    for level_span, dilation, level_bits, offsets_row, query_rows, own_keys, key_value in plans:
        dout_rows = dilate(dout3, dilation, offsets_row)
        log_rows = dilate(log_total, dilation, offsets_row)
        delta_rows = dilate(delta, dilation, offsets_row)
        query_part, key_part, value_part = gradients(
            query_rows, key_value[0], key_value[1], dout_rows, log_rows, delta_rows, factor
        )
        partial_grads = jnp.stack((key_part, value_part))
        if level_span == seq_devices:
            summed = lax.psum_scatter(partial_grads, "seq", scatter_dimension=1, tiled=True)
        else:
            summed = fold_grads(partial_grads, level_bits, position)
        grad_q = grad_q + spread(query_part, dilation, offsets_row)
        grad_k = grad_k + spread(summed[0], dilation, offsets_row)
        grad_v = grad_v + spread(summed[1], dilation, offsets_row)
    flat = (tok_rows, feature_width)
    return (
        attended.reshape(flat),
        grad_q.reshape(flat),
        grad_k.reshape(flat),
        grad_v.reshape(flat),
    )


def solution(mesh):
    return jax.shard_map(
        body,
        mesh=mesh,
        in_specs=(
            P("seq", "rep"),
            P("seq", "rep"),
            P("seq", "rep"),
            P("seq", "rep"),
            P(None, "rep"),
        ),
        out_specs=(P("seq", "rep"), P("seq", "rep"), P("seq", "rep"), P("seq", "rep")),
        check_vma=False,
    )
```

profile of v0, /device:TPU:8, one launch (start us, length us, event | category | flops | bytes accessed | tf_op | source)
XLA Modules:
  0.0 1185.8 jit_solution(8731910405478239539)
XLA Ops:
  7.2 1.6 fusion.145
  16.0 2.2 collective-permute-start
  37.0 3.1 fusion.131
  42.3 2.3 fusion.130
  44.7 183.9 %all_gather.3 = bf16[2,512,2,128]{3,1,2,0:T(8,128)(2,1)S(1)} all-gather(bf16[2,8,2,128]{3,1,2,0:T(8,128)(2,1)S(1)} %pad_maximum_fusion.17), channel_id=1, replica_groups=mesh['seq'=64,'rep'=4] {'seq'}, dimensions={1}, use_global_device_ids=true | all-gather | bytes 532480 | tf_op jit(solution)/shard_map/all_gather | solution.py:157
  235.0 2.2 fusion.127
  237.2 2.2 fusion.132
  239.6 9.5 while.28
  256.5 2.0 reshape_reshape.63
  258.5 1.8 copy.296
  271.3 3.6 collective-permute-start.1
  277.8 2.5 copy.308
  301.1 2.5 copy.299
  305.7 2.6 copy.310
  317.8 2.5 copy.311
  321.2 2.9 fusion.61
  326.4 1.9 convolution_bitcast_fusion.2
  329.5 1.8 fusion.33
  331.2 1.7 fusion.44
  334.7 1.8 convolution_bitcast_fusion.3
  337.4 1.8 fusion.34
  343.4 1.9 convolution_bitcast_fusion.4
  346.3 1.8 fusion.35
  349.8 2.5 copy.301
  352.4 3.5 fusion.49
  355.9 2.5 copy.351
  358.4 78.9 %while.29 = (s32[]{:T(128)}, f32[2,512,2,128]{1,0,3,2:T(2,128)}, f32[2,512,2,128]{1,0,3,2:T(2,128)}, f32[2,512,2,128]{1,0,3,2:T(2,128)}, bf16[2,512,2,128]{3,1,2...) while((s32[]{:T(128)}, f32[2,512,2,128]{1,0,3,2:T(2,128)}, ...), condition=%wide.region_12.13_spmd, body=%wide.region_11.12_spmd.sunk | while | flops 675545088 | bytes 32806212 | solution.py:177
  363.9 10.3 dynamic_update_slice.30
  376.1 10.3 dynamic_update_slice.31
  387.6 10.3 dynamic_update_slice.32
  403.3 10.3 dynamic_update_slice.30
  415.5 10.3 dynamic_update_slice.31
  427.0 10.3 dynamic_update_slice.32
  440.5 2.9 collective-permute-start.8
  444.4 2.2 copy.343
  446.7 2.4 copy.438
  450.6 2.5 copy.330
  453.1 2.4 copy.434
  456.7 2.5 copy.324
  460.3 7.4 collective-permute-start.7
  468.8 2.1 collective-permute-start.9
  471.0 2.8 collective-permute-done.9
  474.0 3.0 collective-permute-start.10
  477.1 3.5 collective-permute-done.10
  483.6 2.5 copy.340
  490.0 674.1 %all-reduce.3.cloned.1.call-done = f32[2,512,2,128]{3,2,0,1:T(2,128)} async-done(((f32[2,512,2,128]{3,2,0,1:T(2,128)}), f32[2,512,2,128]{3,2,0,1:T(2,128)}) %all-reduce.3.cloned.1.call-update) | async-done | bytes 1048592
  1167.7 5.8 fusion.58
  1173.5 2.7 copy.352
  (500 shorter events, 136.5 us)
Async XLA Ops:
  7.2 11.0 copy-start.9
  7.2 1157.0 %all-reduce.3.cloned.1.call-start = ((), (), s32[]{:S(2)}) async-start(), calls=%async_computation | async-start | bytes 2097152
  11.4 9.5 copy-start.8
  16.0 254.3 %collective-permute-start = (bf16[2,128,2,128]{3,1,2,0:T(8,128)(2,1)}, bf16[2,128,2,128]{3,1,2,0:T(8,128)(2,1)}, u32[]{:S(2)}, u32[]{:S(2)}) collective-permute-start(bf16[2,128,2,128]{3,1,2,0:T(8,128)(2,1)} %pad_maximum_fusion.3), channel_id=1, source_target_pairs={{0,4},{4,0},{8,12},{12,8},{16,20},{20,16},{24,28},{28,24},{32,36},... | collective-permute-start | bytes 393224 | tf_op jit(solution)/shard_map/ppermute | solution.py:19
  26.7 228.0 %collective-permute-start.2 = (bf16[2,32,2,128]{3,1,2,0:T(8,128)(2,1)}, bf16[2,32,2,128]{3,1,2,0:T(8,128)(2,1)}, u32[]{:S(2)}, u32[]{:S(2)}) collective-permute-start(bf16[2,32,2,128]{3,1,2,0:T(8,128)(2,1)} %pad_maximum_fusion.10), channel_id=1, source_target_pairs={{0,4},{4,0},{8,12},{12,8},{16,20},{20,16},{24,28},{28,24},{32,36},... | collective-permute-start | bytes 98312 | tf_op jit(solution)/shard_map/ppermute | solution.py:19
  37.0 191.6 %copy-start.16 = (bf16[8,128,2,128]{3,2,1,0:T(2,128)(2,1)S(1)}, bf16[8,128,2,128]{3,2,1,0:T(2,128)(2,1)}, u32[]{:S(2)}) copy-start(bf16[8,128,2,128]{3,2,1,0:T(2,128)(2,1)} %reshape_reshape.66) | copy-start | bytes 1572868
  42.3 187.3 %copy-start.15 = (bf16[8,128,2,128]{3,2,1,0:T(2,128)(2,1)S(1)}, bf16[8,128,2,128]{3,2,1,0:T(2,128)(2,1)}, u32[]{:S(2)}) copy-start(bf16[8,128,2,128]{3,2,1,0:T(2,128)(2,1)} %reshape_reshape.60) | copy-start | bytes 1572868
  249.1 12.5 %copy-start.66 = (f32[2,512,2]{1,2,0:T(2,128)}, f32[2,512,2]{1,2,0:T(2,128)S(1)}, u32[]{:S(2)}) copy-start(f32[2,512,2]{1,2,0:T(2,128)S(1)} %get-tuple-element.97) | copy-start | bytes 24580
  250.0 12.7 %copy-start.82 = (f32[32,2]{0,1:T(2,128)}, f32[32,2]{0,1:T(2,128)S(1)}, u32[]{:S(2)}) copy-start(f32[32,2]{0,1:T(2,128)S(1)} %get-tuple-element.303) | copy-start | bytes 772
  250.0 30.4 %copy-start.88 = (pred[32,2]{0,1:T(4,128)(4,1)}, pred[32,2]{0,1:T(4,128)(4,1)S(1)}, u32[]{:S(2)}) copy-start(pred[32,2]{0,1:T(4,128)(4,1)S(1)} %get-tuple-element.302) | copy-start | bytes 196
  250.7 12.8 %copy-start.90 = (pred[128,2]{0,1:T(4,128)(4,1)}, pred[128,2]{0,1:T(4,128)(4,1)S(1)}, u32[]{:S(2)}) copy-start(pred[128,2]{0,1:T(4,128)(4,1)S(1)} %get-tuple-element.298) | copy-start | bytes 772
  250.7 14.2 %copy-start.84 = (f32[128,2]{0,1:T(2,128)}, f32[128,2]{0,1:T(2,128)S(1)}, u32[]{:S(2)}) copy-start(f32[128,2]{0,1:T(2,128)S(1)} %get-tuple-element.299) | copy-start | bytes 3076
  255.6 14.6 %collective-permute-start.3 = (bf16[2,64,2,128]{3,1,2,0:T(8,128)(2,1)S(1)}, bf16[2,64,2,128]{3,1,2,0:T(8,128)(2,1)S(1)}, u32[]{:S(2)}, u32[]{:S(2)}) collective-permute-start(bf16[2,64,2,128]{3,1,2,0:T(8,128)(2,1)S(1)} %maximum_select_fusion.5), channel_id=1, source_target_pairs={{0,8},{8,0},{4,12},{12,4},{16,24},{24,16},{20,28},{28,20},{32,40},... | collective-permute-start | bytes 196616 | tf_op jit(solution)/shard_map/ppermute | solution.py:19
  262.7 12.3 %copy-start.94 = (s32[2]{0:T(128)S(1)}, s32[2]{0:T(128)}, u32[]{:S(2)}) copy-start(s32[2]{0:T(128)} %get-tuple-element.192) | copy-start | bytes 28
  262.7 57.6 %copy-start.38 = (f32[1024,2]{0,1:T(2,128)}, f32[1024,2]{0,1:T(2,128)S(1)}, u32[]{:S(2)}) copy-start(f32[1024,2]{0,1:T(2,128)S(1)} %mul.587) | copy-start | bytes 24580
  266.4 24.9 %copy-start.36 = (bf16[128,1,1,128]{3,0,2,1:T(8,128)(2,1)}, bf16[128,1,1,128]{3,0,2,1:T(8,128)(2,1)S(1)}, u32[]{:S(2)}) copy-start(bf16[128,1,1,128]{3,0,2,1:T(8,128)(2,1)S(1)} %copy.504) | copy-start | bytes 98308
  266.4 24.9 %copy-start.37 = (bf16[128,1,1,128]{3,0,2,1:T(8,128)(2,1)}, bf16[128,1,1,128]{3,0,2,1:T(8,128)(2,1)S(1)}, u32[]{:S(2)}) copy-start(bf16[128,1,1,128]{3,0,2,1:T(8,128)(2,1)S(1)} %copy.505) | copy-start | bytes 98308
  270.2 18.6 %collective-permute-start.4 = (bf16[2,128,2,128]{3,1,2,0:T(8,128)(2,1)S(1)}, bf16[2,128,2,128]{3,1,2,0:T(8,128)(2,1)S(1)}, u32[]{:S(2)}, u32[]{:S(2)}) collective-permute-start(bf16[2,128,2,128]{3,1,2,0:T(8,128)(2,1)S(1)} %maximum_select_fusion.4), channel_id=1, source_target_pairs={{0,16},{16,0},{4,20},{20,4},{8,24},{24,8},{12,28},{28,12},{32,48},... | collective-permute-start | bytes 393224 | tf_op jit(solution)/shard_map/ppermute | solution.py:19
  271.3 18.7 %collective-permute-start.1 = (bf16[2,256,2,128]{3,1,2,0:T(8,128)(2,1)S(1)}, bf16[2,256,2,128]{3,1,2,0:T(8,128)(2,1)}, u32[]{:S(2)}, u32[]{:S(2)}) collective-permute-start(bf16[2,256,2,128]{3,1,2,0:T(8,128)(2,1)S(1)} %maximum_select_fusion.2), channel_id=1, source_target_pairs={{0,8},{8,0},{4,12},{12,4},{16,24},{24,16},{20,28},{28,20},{32,40},... | collective-permute-start | bytes 786440 | tf_op jit(solution)/shard_map/ppermute | solution.py:19
  276.7 9.7 copy-start.86
  276.7 10.2 copy-start.87
  276.7 10.8 copy-start.95
  289.5 18.7 %collective-permute-start.5 = (bf16[2,256,2,128]{3,1,2,0:T(8,128)(2,1)}, bf16[2,256,2,128]{3,1,2,0:T(8,128)(2,1)}, u32[]{:S(2)}, u32[]{:S(2)}) collective-permute-start(bf16[2,256,2,128]{3,1,2,0:T(8,128)(2,1)} %maximum_select_fusion.3), channel_id=1, source_target_pairs={{0,32},{32,0},{4,36},{36,4},{8,40},{40,8},{12,44},{44,12},{16,48},... | collective-permute-start | bytes 786440 | tf_op jit(solution)/shard_map/ppermute | solution.py:19
  305.6 11.0 copy-start.68
  305.6 11.0 copy-start.69
  305.6 11.0 copy-start.77
  305.7 11.0 copy-start.85
  305.7 11.0 copy-start.91
  310.9 9.4 copy-start.74
  310.9 9.4 copy-start.41
  321.1 11.8 copy-start.75
  325.6 10.9 copy-start.18
  326.4 13.9 %copy-start.32 = (f32[128,8,2]{1,0,2:T(8,128)S(1)}, f32[128,8,2]{1,0,2:T(8,128)}, u32[]{:S(2)}) copy-start(f32[128,8,2]{1,0,2:T(8,128)} %mul.641) | copy-start | bytes 24580
  326.4 13.9 %copy-start.33 = (f32[128,8,2]{1,0,2:T(8,128)S(1)}, f32[128,8,2]{1,0,2:T(8,128)}, u32[]{:S(2)}) copy-start(f32[128,8,2]{1,0,2:T(8,128)} %mul.647) | copy-start | bytes 24580
  386.4 11.5 copy-start.3
  387.0 10.9 copy-start.1
  425.8 11.5 copy-start.3
  426.4 10.9 copy-start.1
  439.7 19.5 %collective-permute-start.6 = (bf16[2,256,2,128]{1,3,2,0:T(8,128)(2,1)}, bf16[2,256,2,128]{1,3,2,0:T(8,128)(2,1)}, u32[]{:S(2)}, u32[]{:S(2)}) collective-permute-start(bf16[2,256,2,128]{1,3,2,0:T(8,128)(2,1)} %select_convert_fusion.1), channel_id=1, source_target_pairs={{0,8},{8,0},{4,12},{12,4},{16,24},{24,16},{20,28},{28,20},{32,40},... | collective-permute-start | bytes 786440 | tf_op jit(solution)/shard_map/ppermute | solution.py:19
  440.5 27.2 %collective-permute-start.8 = (bf16[2,256,2,128]{1,3,2,0:T(8,128)(2,1)}, bf16[2,256,2,128]{1,3,2,0:T(8,128)(2,1)}, u32[]{:S(2)}, u32[]{:S(2)}) collective-permute-start(bf16[2,256,2,128]{1,3,2,0:T(8,128)(2,1)} %select_convert_fusion), channel_id=1, source_target_pairs={{0,32},{32,0},{4,36},{36,4},{8,40},{40,8},{12,44},{44,12},{16,48},... | collective-permute-start | bytes 786440 | tf_op jit(solution)/shard_map/ppermute | solution.py:19
  460.3 10.5 collective-permute-start.7
  468.8 5.1 collective-permute-start.9
  474.0 6.7 collective-permute-start.10
  480.9 5.4 collective-permute-start.11
  490.0 677.4 %copy-start.20 = (f32[32,8,2,512]{3,1,2,0:T(8,128)S(1)}, f32[32,8,2,512]{3,1,2,0:T(8,128)}, u32[]{:S(2)}) copy-start(f32[32,8,2,512]{3,1,2,0:T(8,128)} %copy.438) | copy-start | bytes 3145732
  490.0 677.5 %copy-start.21 = (f32[1024,256]{0,1:T(8,128)S(1)}, f32[1024,256]{0,1:T(8,128)}, u32[]{:S(2)}) copy-start(f32[1024,256]{0,1:T(8,128)} %copy.330) | copy-start | bytes 3145732
  490.0 677.5 %copy-start.40 = (f32[1024,2]{0,1:T(2,128)S(1)}, f32[1024,2]{0,1:T(2,128)}, u32[]{:S(2)}) copy-start(f32[1024,2]{0,1:T(2,128)} %copy-done.38) | copy-start | bytes 24580
  490.0 677.5 %copy-start.43 = (f32[1024,2]{0,1:T(2,128)S(1)}, f32[1024,2]{0,1:T(2,128)}, u32[]{:S(2)}) copy-start(f32[1024,2]{0,1:T(2,128)} %mul.577) | copy-start | bytes 24580
  (68 other events, 272.1 us)
Sparse Core Ops, SparseCore 0:
  446.8 717.3 all-reduce.2
where the time goes:
time: 1200 us; the launch traced here: 1190 us
  waiting for transfers between devices  681 us (57%)
  local copies, waits for them, and re-layouts  203 us (17%)
  blocking collectives  184 us (15%)
  other arithmetic  35.7 us (3%)
  matrix products  31.2 us (3%)
  between operations  28.6 us (2%)
  starting transfers between devices  22.2 us (2%)
    unnamed x2, waiting for transfers between devices  674 us
    all_gather x1, blocking collectives, body(): key_value = lax.all_gather(own_keys, 'seq', axis=1, tiled=True)  184 us
    dynamic_update_slice x14, local copies, waits for them, and re-layouts, body(): lax.map(lambda blocks: attend(blocks[0], blocks[1], blocks[2], factor), (...  68.1 us
    mul x58, local copies, waits for them, and re-layouts, spread(): dilated[:, None] * selector  41.7 us
    unnamed x220, local copies, waits for them, and re-layouts  27.6 us
  transfers between devices with their start and end apart: 13, of which 4 were waited for; matrix products, arithmetic and copies ran while one was open for 10% of the time, Pallas kernels for 0%

commit v1 on v0

v1 whole, which is shorter than its diff:
```python
import jax
import jax.numpy as jnp
from jax import lax
from jax.experimental import pallas as pl
from jax.experimental.pallas import tpu as pltpu
from jax.sharding import PartitionSpec as P

HEADS = 2
KEYS = 512
DIM = 128
TOKENS = 1024
BLOCK = 128
RATES = (8, 32, 128)
FACTOR = DIM**-0.5
MESH = pl.DeviceIdType.MESH
F32 = jnp.float32
BF16 = jnp.bfloat16

WORKER3 = (5, 11)


def dot(a, b, dims):
    return lax.dot_general(a, b, (dims, ((), ())), preferred_element_type=F32)


def nn(a, b):
    return dot(a, b, ((1,), (0,)))


def nt(a, b):
    return dot(a, b, ((1,), (1,)))


def tn(a, b):
    return dot(a, b, ((0,), (0,)))


def split3(a):
    high = a.astype(BF16)
    rest = a - high.astype(F32)
    middle = rest.astype(BF16)
    low = (rest - middle.astype(F32)).astype(BF16)
    return jnp.concatenate([high.astype(F32), middle.astype(F32), low.astype(F32)], 0).astype(BF16)


def join3(a):
    rows = a.shape[0] // 3
    return a[:rows] + a[rows : 2 * rows] + a[2 * rows :]


def select_rows(stats, chooser):
    return join3(nn(split3(stats), chooser))


def select_rows_nt(stats, chooser):
    return join3(nt(split3(stats), chooser))


def iota(shape, dim):
    return lax.broadcasted_iota(jnp.int32, shape, dim)


def kernel(
    offsets, query, keys, values, dout,
    att_out, dq_out, dk_out, dv_out,
    sel, spread, sel2, sel3, dout_t, powers0, weighted0, stat0, logs,
    pack1, pack2, pack3, in1, work, in3, power_item, stat_item, weighted1,
    send2, send3, back2, back3, grad_send2, grad_send3, grad1, grad2, grad3,
    tiles, tiles1, tiles2, tiles3,
    send_in, send_back, send_stat, send_grad,
    recv_in, recv_back, recv_stat, recv_grad,
):
    me = lax.axis_index("seq")
    y = lax.rem(me, 4)
    z = lax.rem(lax.div(me, 4), 4)
    x = lax.div(me, 16)
    place = lax.rem(me, 16)
    plane = me - place
    group = me - y
    is2 = lax.rem(y, 2) == 0
    is3 = (place == WORKER3[0]) | (place == WORKER3[1])
    one2 = jnp.where(is2, 1, 0)
    one3 = jnp.where(is3, 1, 0)

    barrier = pltpu.get_barrier_semaphore()

    def greet(device):
        pl.semaphore_signal(barrier, inc=1, device_id={"seq": device}, device_id_type=MESH)

    @pl.when(is3)
    def _():
        def step(i, carry):
            greet(lax.rem(me + i, 64))
            return carry

        lax.fori_loop(1, 64, step, 0)

    @pl.when(is2)
    def _():
        def step(i, carry):
            greet(plane + lax.rem(place + i, 16))
            return carry

        lax.fori_loop(1, 16, step, 0)

    for spot in WORKER3:
        @pl.when(place != spot)
        def _(spot=spot):
            greet(plane + spot)

    for i in range(1, 4):
        greet(group + lax.rem(y + i, 4))

    bases = (0, 32 * y, 8 * place)
    for head in range(HEADS):
        off = [offsets[level, head] for level in range(3)]
        row = iota((256, 1), 0)
        target = jnp.where(
            row < 128,
            row * RATES[0] + off[0],
            jnp.where(row < 160, (row - 128) * RATES[1] + off[1], (row - 160) * RATES[2] + off[2]),
        )
        sel[head] = jnp.where(iota((256, TOKENS), 1) == target, 1.0, 0.0).astype(BF16)
        column = iota((1, 256), 1)
        target = jnp.where(
            column < 128,
            column * RATES[0] + off[0],
            jnp.where(
                column < 160, (column - 128) * RATES[1] + off[1], (column - 160) * RATES[2] + off[2]
            ),
        )
        spread[head] = jnp.where(iota((TOKENS, 256), 0) == target, 1.0, 0.0).astype(BF16)
        row = iota((128, 1), 0)
        for ref, level in ((sel2, 1), (sel3, 2)):
            target = (row - bases[level]) * RATES[level] + off[level]
            ref[head] = jnp.where(iota((128, TOKENS), 1) == target, 1.0, 0.0).astype(BF16)

        lanes = slice(DIM * head, DIM * head + DIM)
        chooser = sel[head, 0:176]
        pair_qk = nn(chooser, jnp.concatenate([query[:, lanes], keys[:, lanes]], 1))
        pair_vd = nn(chooser, jnp.concatenate([values[:, lanes], dout[:, lanes]], 1))
        pack1[:, 512 * head : 512 * head + 256] = pair_qk[:128].astype(BF16)
        pack1[:, 512 * head + 256 : 512 * head + 512] = pair_vd[:128].astype(BF16)
        pack2[head, :, 0:256] = pair_qk[128:160].astype(BF16)
        pack2[head, :, 256:512] = pair_vd[128:160].astype(BF16)
        pack3[head] = jnp.concatenate([pair_qk[160:168], pair_vd[160:168]], 0).astype(BF16)

    pl.semaphore_wait(barrier, 3 + (8 - one2) + (8 - one3) + 15 * one3)

    def remote(src, dst, send_sem, recv_sem, device):
        return pltpu.make_async_remote_copy(
            src_ref=src, dst_ref=dst, send_sem=send_sem, recv_sem=recv_sem,
            device_id={"seq": device}, device_id_type=MESH,
        )

    pending = []

    def send(src, dst, send_sem, recv_sem, device):
        copy = remote(src, dst, send_sem, recv_sem, device)
        pending.append((device, copy))

        @pl.when(device != me)
        def _():
            copy.start()

    def arrived(ref, sem):
        pltpu.make_async_copy(ref, ref, sem).wait()

    for block in range(4):
        for head in range(HEADS):
            send(pack3.at[head], in3.at[me], send_in.at[2 * block + head], recv_in.at[2],
                 16 * block + WORKER3[head])
    for block in range(4):
        for head in range(HEADS):
            send(pack2.at[head], work.at[pl.ds(pl.multiple_of(32 * place, 32), 32)],
                 send_in.at[8 + 2 * block + head], recv_in.at[1], plane + 4 * block + 2 * head)
    for i in range(1, 4):
        send(pack1, in1.at[pl.ds(pl.multiple_of(128 * y, 128), 128)], send_in.at[15 + i],
             recv_in.at[0], group + lax.rem(y + i, 4))

    in1[pl.ds(pl.multiple_of(128 * y, 128), 128)] = pack1[...]
    for head in range(HEADS):
        @pl.when(place == WORKER3[head])
        def _(head=head):
            in3[me] = pack3[head]

        @pl.when(y == 2 * head)
        def _(head=head):
            work[pl.ds(pl.multiple_of(32 * place, 32), 32)] = pack2[head]

    def unit_refs(unit):
        head = lax.div(unit, 2)
        segment = lax.rem(unit, 2)
        return head, segment, pl.ds(pl.multiple_of(DIM * head, DIM), DIM)

    def forward0(unit, carry):
        head, segment, lanes = unit_refs(unit)
        rows = pl.ds(pl.multiple_of(KEYS * segment, KEYS), KEYS)
        key, value = keys[rows, lanes], values[rows, lanes]
        for chunk in range(2):
            start = pl.multiple_of(KEYS * segment + 256 * chunk, 256)
            part = pl.ds(start, 256)
            scores = nt(key, query[part, lanes]) * FACTOR
            row_max = jnp.max(scores, 0, keepdims=True)
            powers = jnp.exp(scores - row_max)
            powers0[unit, :, 256 * chunk : 256 * chunk + 256] = powers
            weighted0[head, :, part] = tn(value, powers.astype(BF16))
            stat0[head, 0:1, part] = row_max
            stat0[head, 1:2, part] = jnp.sum(powers, 0, keepdims=True)
        return carry

    lax.fori_loop(0, 4, forward0, 0)
    for head in range(HEADS):
        dout_t[head] = dout[:, DIM * head : DIM * head + DIM].astype(F32).T

    def item_forward(ref, first, block, slot):
        rows = pl.ds(pl.multiple_of(BLOCK * block, BLOCK), BLOCK)
        scores = nt(ref[:, first + 128 : first + 256], ref[rows, first : first + 128]) * FACTOR
        row_max = jnp.max(scores, 0, keepdims=True)
        powers = jnp.exp(scores - row_max)
        total = jnp.sum(powers, 0, keepdims=True)
        power_item[slot] = powers
        stat_item[slot] = jnp.concatenate([row_max, total, jnp.zeros((6, BLOCK), F32)], 0)
        return tn(powers.astype(BF16), ref[:, first + 256 : first + 384])

    def item_backward(ref, first, block, slot, log_all, delta_all, log_own, delta_own):
        rows = pl.ds(pl.multiple_of(BLOCK * block, BLOCK), BLOCK)
        q_all, k_all = ref[:, first : first + 128], ref[:, first + 128 : first + 256]
        v_all, d_all = ref[:, first + 256 : first + 384], ref[:, first + 384 : first + 512]
        k_own, v_own = ref[rows, first + 128 : first + 256], ref[rows, first + 256 : first + 384]
        d_own = ref[rows, first + 384 : first + 512]
        probs = power_item[slot] * jnp.exp(stat_item[slot, 0:1] - log_own)
        low = (probs * (nt(v_all, d_own) - delta_own)).astype(BF16)
        grad_q = FACTOR * tn(low, k_all)
        probs = jnp.exp(nt(k_own, q_all) * FACTOR - log_all)
        low = (probs * (nt(v_own, d_all) - delta_all)).astype(BF16)
        grad_k = FACTOR * nn(low, q_all)
        grad_v = nn(probs.astype(BF16), d_all)
        return jnp.concatenate([grad_q, grad_k, grad_v], 1)

    worker_block = jnp.where(is2, z, x)
    worker_head = jnp.where(is2, lax.div(y, 2), jnp.where(place == WORKER3[0], 0, 1))

    @pl.when(is2)
    def _():
        arrived(work.at[pl.ds(0, 480)], recv_in.at[1])

    @pl.when(is3)
    def _():
        arrived(in3.at[pl.ds(0, 63)], recv_in.at[2])
        both = in3[...].astype(F32)
        work[:, 0:256] = both[:, 0:8].reshape(KEYS, 256).astype(BF16)
        work[:, 256:512] = both[:, 8:16].reshape(KEYS, 256).astype(BF16)

    @pl.when(is2 | is3)
    def _():
        weighted = item_forward(work, 0, worker_block, 2)
        stats = stat_item[2]

        @pl.when(is2)
        def _():
            for i in range(4):
                send2[i] = jnp.concatenate([weighted[32 * i : 32 * i + 32], stats], 0)

        @pl.when(is3)
        def _():
            for i in range(16):
                send3[i] = jnp.concatenate([weighted[8 * i : 8 * i + 8], stats], 0)

    def returns(src2, dst2, src3, dst3, sems, recv, wait):
        def each(src, dst, sem, recv_sem, device):
            copy = remote(src, dst, sem, recv_sem, device)
            if wait:
                copy.wait_send()
            else:
                copy.start()

        @pl.when(is2)
        def _():
            for i in range(1, 4):
                other = lax.rem(y + i, 4)
                each(src2.at[other], dst2.at[worker_head], sems.at[i], recv.at[worker_head], group + other)
            if not wait:
                dst2[worker_head] = src2[y]

        @pl.when(is3)
        def _():
            def step(i, carry):
                other = lax.rem(place + i, 16)
                each(src3.at[other], dst3.at[worker_head], sems.at[i], recv.at[2 + worker_head], plane + other)
                return carry

            lax.fori_loop(1, 16, step, 0)
            if not wait:
                dst3[worker_head] = src3[place]

    def returned(dst2, dst3, recv):
        for head in range(HEADS):
            @pl.when(y != 2 * head)
            def _(head=head):
                arrived(dst2.at[head], recv.at[head])

            @pl.when(place != WORKER3[head])
            def _(head=head):
                arrived(dst3.at[head], recv.at[2 + head])

    returns(send2, back2, send3, back3, send_back, recv_back, False)

    arrived(in1.at[pl.ds(0, 384)], recv_in.at[0])
    for head in range(HEADS):
        weighted1[head] = item_forward(in1, 512 * head, y, head)

    returned(back2, back3, recv_back)
    position = iota((1, TOKENS), 1)
    for head in range(HEADS):
        found = (
            select_rows(stat_item[head], sel[head, 0:128]),
            select_rows(back2[head, 32:40], sel2[head]),
            select_rows(back3[head, 8:16], sel3[head]),
        )
        maxima = [stat0[head, 0:1]]
        for level in range(3):
            member = lax.rem(position, RATES[level]) == offsets[level, head]
            maxima.append(jnp.where(member, found[level][0:1], -jnp.inf))
        peak = jnp.maximum(jnp.maximum(maxima[0], maxima[1]), jnp.maximum(maxima[2], maxima[3]))
        factors = [jnp.exp(item - peak) for item in maxima]
        denominator = factors[0] * stat0[head, 1:2]
        for level in range(3):
            denominator += factors[level + 1] * found[level][1:2]
        log_total = peak + jnp.log(denominator)
        shares = [item / denominator for item in factors]
        lane_shares = select_rows_nt(
            jnp.concatenate(shares[1:] + [jnp.zeros((5, TOKENS), F32)], 0), sel[head]
        )
        lane = iota((1, 256), 1)
        share = jnp.where(lane < 128, lane_shares[0:1], jnp.where(lane < 160, lane_shares[1:2], lane_shares[2:3]))
        stacked = jnp.concatenate(
            [weighted1[head], back2[head, 0:32], back3[head, 0:8], jnp.zeros((88, DIM), F32)], 0
        ).T * share
        high = stacked.astype(BF16)
        low = (stacked - high.astype(F32)).astype(BF16)
        attended = shares[0] * weighted0[head] + nn(high, sel[head]) + nn(low, sel[head])
        delta = jnp.sum(dout_t[head] * attended, 0, keepdims=True)
        att_out[:, DIM * head : DIM * head + DIM] = attended.T
        rows = jnp.concatenate([log_total, delta, jnp.zeros((6, TOKENS), F32)], 0)
        logs[head] = rows
        tiles[0, 2 * head : 2 * head + 2] = select_rows_nt(rows, sel[head, 0:128])[0:2]
        tiles[1, 2 * head : 2 * head + 2] = select_rows_nt(rows, sel2[head])[0:2]
        tiles[2, 2 * head : 2 * head + 2] = select_rows_nt(rows, sel3[head])[0:2]
    for level in range(3):
        tiles[level, 4:8] = jnp.zeros((4, BLOCK), F32)

    for block in range(4):
        for head in range(HEADS):
            send(tiles.at[2], tiles3.at[me], send_stat.at[2 * block + head], recv_stat.at[2],
                 16 * block + WORKER3[head])
    for block in range(4):
        for head in range(HEADS):
            send(tiles.at[1], tiles2.at[place], send_stat.at[8 + 2 * block + head], recv_stat.at[1],
                 plane + 4 * block + 2 * head)
    for i in range(1, 4):
        send(tiles.at[0], tiles1.at[y], send_stat.at[15 + i], recv_stat.at[0], group + lax.rem(y + i, 4))
    tiles1[y] = tiles[0]

    @pl.when(is2)
    def _():
        tiles2[place] = tiles[1]

    @pl.when(is3)
    def _():
        tiles3[me] = tiles[2]

    def backward0(unit, carry):
        head, segment, lanes = unit_refs(unit)
        rows = pl.ds(pl.multiple_of(KEYS * segment, KEYS), KEYS)
        key, value = keys[rows, lanes], values[rows, lanes]
        grad_k = jnp.zeros((KEYS, DIM), F32)
        grad_v = jnp.zeros((KEYS, DIM), F32)
        for chunk in range(2):
            part = pl.ds(pl.multiple_of(KEYS * segment + 256 * chunk, 256), 256)
            rescale = jnp.exp(stat0[head, 0:1, part] - logs[head, 0:1, part])
            probs = powers0[unit, :, 256 * chunk : 256 * chunk + 256] * rescale
            grad_rows = dout[part, lanes]
            low = (probs * (nt(value, grad_rows) - logs[head, 1:2, part])).astype(BF16)
            grad_k += nn(low, query[part, lanes])
            grad_v += nn(probs.astype(BF16), grad_rows)
            dq_out[part, lanes] = (FACTOR * tn(key, low)).T
        dk_out[rows, lanes] = FACTOR * grad_k
        dv_out[rows, lanes] = grad_v
        return carry

    lax.fori_loop(0, 4, backward0, 0)

    def row_blocks(blocks):
        first = worker_head == 0
        logs_all = [jnp.where(first, blocks[i, 0:1], blocks[i, 2:3]) for i in range(4)]
        deltas_all = [jnp.where(first, blocks[i, 1:2], blocks[i, 3:4]) for i in range(4)]
        return logs_all, deltas_all

    def pick(rows, block):
        chosen = rows[0]
        for i in range(1, 4):
            chosen = jnp.where(block == i, rows[i], chosen)
        return chosen

    @pl.when(is2)
    def _():
        arrived(tiles2.at[pl.ds(0, 15)], recv_stat.at[1])
        stat_item[3] = jnp.sum(tiles2[0:4], 0)
        for i in range(1, 4):
            stat_item[3 + i] = jnp.sum(tiles2[4 * i : 4 * i + 4], 0)

    @pl.when(is3)
    def _():
        arrived(tiles3.at[pl.ds(0, 63)], recv_stat.at[2])
        for i in range(4):
            stat_item[3 + i] = jnp.sum(tiles3[16 * i : 16 * i + 16], 0)

    @pl.when(is2 | is3)
    def _():
        log_rows, delta_rows = row_blocks(stat_item[3:7])
        grads = item_backward(
            work, 0, worker_block, 2,
            jnp.concatenate(log_rows, 1), jnp.concatenate(delta_rows, 1),
            pick(log_rows, worker_block), pick(delta_rows, worker_block),
        )

        @pl.when(is2)
        def _():
            for i in range(4):
                grad_send2[i] = grads[32 * i : 32 * i + 32]

        @pl.when(is3)
        def _():
            for i in range(16):
                grad_send3[i] = grads[8 * i : 8 * i + 8]

    returns(grad_send2, grad2, grad_send3, grad3, send_grad, recv_grad, False)

    arrived(tiles1.at[pl.ds(0, 3)], recv_stat.at[0])
    for head in range(HEADS):
        log_rows = [tiles1[i, 2 * head : 2 * head + 1] for i in range(4)]
        delta_rows = [tiles1[i, 2 * head + 1 : 2 * head + 2] for i in range(4)]
        grad1[head] = item_backward(
            in1, 512 * head, y, head,
            jnp.concatenate(log_rows, 1), jnp.concatenate(delta_rows, 1),
            tiles[0, 2 * head : 2 * head + 1], tiles[0, 2 * head + 1 : 2 * head + 2],
        )

    returned(grad2, grad3, recv_grad)
    for head in range(HEADS):
        lanes = slice(DIM * head, DIM * head + DIM)
        stacked = jnp.concatenate(
            [grad1[head], grad2[head], grad3[head], jnp.zeros((88, 3 * DIM), F32)], 0
        ).astype(BF16)
        added = nn(spread[head], stacked)
        dq_out[:, lanes] += added[:, 0:128]
        dk_out[:, lanes] += added[:, 128:256]
        dv_out[:, lanes] += added[:, 256:384]

    for device, copy in pending:
        @pl.when(device != me)
        def _(copy=copy):
            copy.wait_send()
    returns(send2, back2, send3, back3, send_back, recv_back, True)
    returns(grad_send2, grad2, grad_send3, grad3, send_grad, recv_grad, True)


def body(query, keys, values, grad_out, offsets):
    vmem = pl.BlockSpec(memory_space=pltpu.VMEM)
    smem = pl.BlockSpec(memory_space=pltpu.SMEM)
    out = jax.ShapeDtypeStruct((TOKENS, HEADS * DIM), F32)
    dma = pltpu.SemaphoreType.DMA
    return pl.pallas_call(
        kernel,
        out_shape=(out, out, out, out),
        in_specs=[smem, vmem, vmem, vmem, vmem],
        out_specs=(vmem, vmem, vmem, vmem),
        scratch_shapes=[
            pltpu.VMEM((2, 256, TOKENS), BF16),
            pltpu.VMEM((2, TOKENS, 256), BF16),
            pltpu.VMEM((2, 128, TOKENS), BF16),
            pltpu.VMEM((2, 128, TOKENS), BF16),
            pltpu.VMEM((2, DIM, TOKENS), F32),
            pltpu.VMEM((4, KEYS, KEYS), F32),
            pltpu.VMEM((2, DIM, TOKENS), F32),
            pltpu.VMEM((2, 8, TOKENS), F32),
            pltpu.VMEM((2, 8, TOKENS), F32),
            pltpu.VMEM((128, 1024), BF16),
            pltpu.VMEM((2, 32, 512), BF16),
            pltpu.VMEM((2, 16, 256), BF16),
            pltpu.VMEM((512, 1024), BF16),
            pltpu.VMEM((512, 512), BF16),
            pltpu.VMEM((64, 16, 256), BF16),
            pltpu.VMEM((3, 512, 128), F32),
            pltpu.VMEM((7, 8, 128), F32),
            pltpu.VMEM((2, 128, 128), F32),
            pltpu.VMEM((4, 40, 128), F32),
            pltpu.VMEM((16, 16, 128), F32),
            pltpu.VMEM((2, 40, 128), F32),
            pltpu.VMEM((2, 16, 128), F32),
            pltpu.VMEM((4, 32, 384), F32),
            pltpu.VMEM((16, 8, 384), F32),
            pltpu.VMEM((2, 128, 384), F32),
            pltpu.VMEM((2, 32, 384), F32),
            pltpu.VMEM((2, 8, 384), F32),
            pltpu.VMEM((3, 8, 128), F32),
            pltpu.VMEM((4, 8, 128), F32),
            pltpu.VMEM((16, 8, 128), F32),
            pltpu.VMEM((64, 8, 128), F32),
            dma((19,)),
            dma((16,)),
            dma((19,)),
            dma((16,)),
            dma((3,)),
            dma((4,)),
            dma((3,)),
            dma((4,)),
        ],
        compiler_params=pltpu.CompilerParams(
            collective_id=0, has_side_effects=True, vmem_limit_bytes=48 * 2**20
        ),
    )(offsets, query, keys, values, grad_out)


def solution(mesh):
    spec = P("seq", "rep")
    return jax.shard_map(
        body,
        mesh=mesh,
        in_specs=(spec, spec, spec, spec, P(None, "rep")),
        out_specs=(spec, spec, spec, spec),
        check_vma=False,
    )
```

time: 1200 us -> 53.3 us (0.04); the launches traced: 1190 us -> 53 us
  waiting for transfers between devices: 681 us -> 0 us
  local copies, waits for them, and re-layouts: 203 us -> 9.44 us
  blocking collectives: 184 us -> 0 us
  Pallas kernels: 0 us -> 42.9 us
  other arithmetic: 35.7 us -> 0 us
  matrix products: 31.2 us -> 0 us
  between operations: 28.6 us -> 0.65 us
  starting transfers between devices: 22.2 us -> 0 us
    unnamed x2 -> x0, waiting for transfers between devices: 674 us -> none
    all_gather x1 -> x0, blocking collectives: 184 us -> none  [body(): key_value = lax.all_gather(own_keys, 'seq', axis=1, tiled=True)]
    dynamic_update_slice x14 -> x0, local copies, waits for them, and re-layouts: 68.1 us -> none  [body(): lax.map(lambda blocks: attend(blocks[0], blocks[1], blocks[2], factor), (...]
    pallas_call x0 -> x1, Pallas kernels: none -> 42.9 us  [body(): pl.pallas_call(kernel, out_shape=(out, out, out, out), in_specs=[smem, vm...]
    mul x61 -> x0, local copies, waits for them, and re-layouts: 42 us -> none  [the longest x58 41.7 us: spread(): dilated[:, None] * selector]
    dot_general x32 -> x0, matrix products: 31.2 us -> none  [the longest x5 7.97 us: gradients(): jnp.einsum('hqk,qhd->khd', grad_low, query_rows, preferred_element_type=j...]
    ppermute x12 -> x0, starting transfers between devices: 22.1 us -> none  [partner_2(): return lax.ppermute(block, axis, route)]
    slice x20 -> x0, local copies, waits for them, and re-layouts: 21.1 us -> none  [the longest x18 18.7 us: dilate(): folded[:, :, head]]
  transfers between devices with their start and end apart: 13 -> 0, of which waited for: 4 -> 0; matrix products, arithmetic and copies ran while one was open for 10% -> 0% of each run, Pallas kernels for 0% -> 0%
where the time goes in v1:
time: 53.3 us; the launch traced here: 53 us
  Pallas kernels  42.9 us (80%)
  local copies, waits for them, and re-layouts  9.44 us (18%)
  between operations  0.65 us (1%)
    pallas_call x1, Pallas kernels, body(): pl.pallas_call(kernel, out_shape=(out, out, out, out), in_specs=[smem, vm...  42.9 us
    unnamed x15, local copies, waits for them, and re-layouts  9.44 us

profile of v1, /device:TPU:8, one launch (start us, length us, event | category | flops | bytes accessed | tf_op | source)
XLA Modules:
  0.0 53.0 jit_solution(12804446709326650157)
XLA Ops:
  0.6 0.8 %copy.9.offsets = s32[3,2]{1,0:T(4,128)S(1)} copy(s32[3,2]{0,1:T(2,128)} %param.9) | data formatting | bytes 48 | tf_op args[4]
  1.4 0.0 copy-start
  1.4 1.0 %copy-done = bf16[1024,256]{1,0:T(8,128)(2,1)S(1)} copy-done((bf16[1024,256]{1,0:T(8,128)(2,1)S(1)}, bf16[1024,256]{1,0:T(8,128)(2,1)}, u32[]{:S(2)}) %copy-start) | copy-done | bytes 524312
  2.4 0.0 copy-start.1
  2.4 1.0 %copy-done.1 = bf16[1024,256]{1,0:T(8,128)(2,1)S(1)} copy-done((bf16[1024,256]{1,0:T(8,128)(2,1)S(1)}, bf16[1024,256]{1,0:T(8,128)(2,1)}, u32[]{:S(2)}) %copy-start.1) | copy-done | bytes 524312
  3.5 0.0 copy-start.2
  3.5 1.0 %copy-done.2 = bf16[1024,256]{1,0:T(8,128)(2,1)S(1)} copy-done((bf16[1024,256]{1,0:T(8,128)(2,1)S(1)}, bf16[1024,256]{1,0:T(8,128)(2,1)}, u32[]{:S(2)}) %copy-start.2) | copy-done | bytes 524312
  4.5 0.0 copy-start.3
  4.5 1.0 %copy-done.3 = bf16[1024,256]{1,0:T(8,128)(2,1)S(1)} copy-done((bf16[1024,256]{1,0:T(8,128)(2,1)S(1)}, bf16[1024,256]{1,0:T(8,128)(2,1)}, u32[]{:S(2)}) %copy-start.3) | copy-done | bytes 524312
  5.6 42.9 %shard_map.84 = (f32[1024,256]{1,0:T(8,128)S(1)}, f32[1024,256]{1,0:T(8,128)S(1)}, f32[1024,256]{1,0:T(8,128)S(1)}, f32[1024,256]{1,0:T(8,128)}) custom-call(s32[3,2]{1,0:T(4,128)S(1)} %copy.9.offsets, bf16[1024,256]{1,0:T(8,128)(2,1)S(1)} %copy-done, bf16[1024,256]{1,0:T(8,128)(2,1)S(1)} %copy-done.1, bf16[1024,256]{1,0:T(8,128)(2,1)S(1)} %copy-done.2, ...), custom_call_target="tpu_custom_call" | custom-call | tf_op jit(solution)/shard_map/pallas_call | solution.py:474
  48.5 1.0 %copy.14 = f32[1024,256]{1,0:T(8,128)} copy(f32[1024,256]{1,0:T(8,128)S(1)} %get-tuple-element.8) | data formatting | bytes 2097152
  49.5 1.0 %copy.15 = f32[1024,256]{1,0:T(8,128)} copy(f32[1024,256]{1,0:T(8,128)S(1)} %get-tuple-element.9) | data formatting | bytes 2097152
  50.4 0.0 copy-start.4
  50.4 1.0 %copy.16 = f32[1024,256]{1,0:T(8,128)} copy(f32[1024,256]{1,0:T(8,128)S(1)} %get-tuple-element.10) | data formatting | bytes 2097152
  51.4 0.6 %copy-done.4 = f32[1024,256]{1,0:T(8,128)S(1)} copy-done((f32[1024,256]{1,0:T(8,128)S(1)}, f32[1024,256]{1,0:T(8,128)}, u32[]{:S(2)}) %copy-start.4) | copy-done | bytes 1048600
  52.0 1.0 %copy.17 = f32[1024,256]{1,0:T(8,128)} copy(f32[1024,256]{1,0:T(8,128)S(1)} %copy-done.4) | data formatting | bytes 2097152
Async XLA Ops:
  1.4 1.0 %copy-start = (bf16[1024,256]{1,0:T(8,128)(2,1)S(1)}, bf16[1024,256]{1,0:T(8,128)(2,1)}, u32[]{:S(2)}) copy-start(bf16[1024,256]{1,0:T(8,128)(2,1)} %query.1) | copy-start | bytes 1572868
  2.4 1.0 %copy-start.1 = (bf16[1024,256]{1,0:T(8,128)(2,1)S(1)}, bf16[1024,256]{1,0:T(8,128)(2,1)}, u32[]{:S(2)}) copy-start(bf16[1024,256]{1,0:T(8,128)(2,1)} %keys.1) | copy-start | bytes 1572868
  3.5 1.0 %copy-start.2 = (bf16[1024,256]{1,0:T(8,128)(2,1)S(1)}, bf16[1024,256]{1,0:T(8,128)(2,1)}, u32[]{:S(2)}) copy-start(bf16[1024,256]{1,0:T(8,128)(2,1)} %values.1) | copy-start | bytes 1572868
  4.5 1.0 %copy-start.3 = (bf16[1024,256]{1,0:T(8,128)(2,1)S(1)}, bf16[1024,256]{1,0:T(8,128)(2,1)}, u32[]{:S(2)}) copy-start(bf16[1024,256]{1,0:T(8,128)(2,1)} %dout.1) | copy-start | bytes 1572868
  50.4 1.6 %copy-start.4 = (f32[1024,256]{1,0:T(8,128)S(1)}, f32[1024,256]{1,0:T(8,128)}, u32[]{:S(2)}) copy-start(f32[1024,256]{1,0:T(8,128)} %get-tuple-element.11) | copy-start | bytes 3145732

commit v2 on v1

v2 whole, which is shorter than its diff:
```python
import jax
import jax.numpy as jnp
from jax import lax
from jax.experimental import pallas as pl
from jax.experimental.pallas import tpu as pltpu
from jax.sharding import PartitionSpec as P

HEADS = 2
KEYS = 512
DIM = 128
TOKENS = 1024
BLOCK = 128
RATES = (8, 32, 128)
FACTOR = DIM**-0.5
MESH = pl.DeviceIdType.MESH
F32 = jnp.float32
BF16 = jnp.bfloat16

WORKER3 = (5, 11)


def dot(a, b, dims):
    return lax.dot_general(a, b, (dims, ((), ())), preferred_element_type=F32)


def nn(a, b):
    return dot(a, b, ((1,), (0,)))


def nt(a, b):
    return dot(a, b, ((1,), (1,)))


def tn(a, b):
    return dot(a, b, ((0,), (0,)))


def split3(a):
    high = a.astype(BF16)
    rest = a - high.astype(F32)
    middle = rest.astype(BF16)
    low = (rest - middle.astype(F32)).astype(BF16)
    return jnp.concatenate([high.astype(F32), middle.astype(F32), low.astype(F32)], 0).astype(BF16)


def join3(a):
    rows = a.shape[0] // 3
    return a[:rows] + a[rows : 2 * rows] + a[2 * rows :]


def select_rows(stats, chooser):
    return join3(nn(split3(stats), chooser))


def select_rows_nt(stats, chooser):
    return join3(nt(split3(stats), chooser))


def iota(shape, dim):
    return lax.broadcasted_iota(jnp.int32, shape, dim)


def worker2(half, head):
    return 4 * (1 + half) + 2 * head


def kernel(
    offsets, query_hbm, keys_hbm, values_hbm, dout_hbm,
    att_out, dq_out, dk_out, dv_out, spread, stack_out,
    query, keys, values, dout,
    sel, sel2, sel3, dout_t, powers0, weighted0, stat0, logs,
    pack1, pack2, pack3, in1, work, in3, power1, power_work, stat1, stat_own,
    send1, send2, send3, back1, back2, back3, grad_send1, grad_send2, grad_send3, stack,
    tiles, tiles1, tiles2, tiles3,
    load_sem, send_in, send_back, send_stat, send_grad,
    recv_in, recv_back, recv_stat, recv_grad,
):
    me = lax.axis_index("seq")
    y = lax.rem(me, 4)
    z = lax.rem(lax.div(me, 4), 4)
    x = lax.div(me, 16)
    place = lax.rem(me, 16)
    plane = me - place
    group = me - y
    side = lax.rem(y, 2)
    pair = lax.div(y, 2)
    partner = group + 2 * pair + 1 - side
    half = lax.div(z, 2)
    is2 = (side == 0) & ((z == 1) | (z == 2))
    head2 = pair
    is3 = (place == WORKER3[0]) | (place == WORKER3[1])
    head3 = jnp.where(place == WORKER3[0], 0, 1)
    one2 = jnp.where(is2, 1, 0)
    one3 = jnp.where(is3, 1, 0)

    loads = []
    for i, (source, held) in enumerate(
        ((query_hbm, query), (keys_hbm, keys), (values_hbm, values), (dout_hbm, dout))
    ):
        loads.append(pltpu.make_async_copy(source, held, load_sem.at[i]))
        loads[-1].start()

    barrier = pltpu.get_barrier_semaphore()

    def greet(device):
        pl.semaphore_signal(barrier, inc=1, device_id={"seq": device}, device_id_type=MESH)

    @pl.when(is3)
    def _():
        def step(i, carry):
            greet(lax.rem(me + i, 64))
            return carry

        lax.fori_loop(1, 64, step, 0)

    @pl.when(is2)
    def _():
        def step(i, carry):
            greet(plane + lax.rem(place + i, 16))
            return carry

        lax.fori_loop(1, 16, step, 0)

    for spot in WORKER3:
        @pl.when(place != spot)
        def _(spot=spot):
            greet(plane + spot)
    for head in range(HEADS):
        spot = worker2(half, head)

        @pl.when(place != spot)
        def _(spot=spot):
            greet(plane + spot)

    for i in range(1, 4):
        greet(group + lax.rem(y + i, 4))

    bases = (0, 32 * y, 8 * place)
    for head in range(HEADS):
        off = [offsets[head, level] for level in range(3)]

        def target(index, off=off):
            return jnp.where(
                index < 128,
                index * RATES[0] + off[0],
                jnp.where(
                    index < 160, (index - 128) * RATES[1] + off[1], (index - 160) * RATES[2] + off[2]
                ),
            )

        sel[head] = jnp.where(
            iota((256, TOKENS), 1) == target(iota((256, 1), 0)), 1.0, 0.0
        ).astype(BF16)
    for load in loads:
        load.wait()
    for head in range(HEADS):
        lanes = slice(DIM * head, DIM * head + DIM)
        chooser = sel[head, 0:176]
        first = nn(chooser, jnp.concatenate([keys[:, lanes], values[:, lanes]], 1))
        second = nn(chooser, jnp.concatenate([query[:, lanes], dout[:, lanes]], 1))
        pack1[head, :, 0:256] = first[:128].astype(BF16)
        pack1[head, :, 256:512] = second[:128].astype(BF16)
        pack2[head, :, 0:256] = first[128:160].astype(BF16)
        pack2[head, :, 256:512] = second[128:160].astype(BF16)
        pack3[head] = jnp.concatenate([first[160:168], second[160:168]], 0).astype(BF16)

    pl.semaphore_wait(barrier, 3 + (4 - one2) + (8 - one3) + 15 * one3 + 7 * one2)

    def remote(src, dst, send_sem, recv_sem, device):
        return pltpu.make_async_remote_copy(
            src_ref=src, dst_ref=dst, send_sem=send_sem, recv_sem=recv_sem,
            device_id={"seq": device}, device_id_type=MESH,
        )

    pending = []

    def send(src, dst, send_sem, recv_sem, device):
        copy = remote(src, dst, send_sem, recv_sem, device)
        pending.append((device, copy))

        @pl.when(device != me)
        def _():
            copy.start()

    def arrived(ref, sem):
        pltpu.make_async_copy(ref, ref, sem).wait()

    mine1 = pl.ds(pl.multiple_of(128 * y, 128), 128)
    mine2 = pl.ds(pl.multiple_of(32 * place, 32), 32)
    for block in range(4):
        for head in range(HEADS):
            send(pack3.at[head], in3.at[me], send_in.at[2 * block + head], recv_in.at[4],
                 16 * block + WORKER3[head])
    for part in range(2):
        for i in range(4):
            lanes = (slice(0, 384), slice(384, 512))[part]
            send(pack2.at[i % 2, :, lanes], work.at[mine2, lanes], send_in.at[8 + 4 * part + i],
                 recv_in.at[2 + part], plane + worker2(i // 2, i % 2))
        for i in range(3):
            wide = 384 if i == 0 else 256
            lanes = (slice(0, wide), slice(wide, 512))[part]
            other = (partner, group + 2 * (1 - pair), group + 2 * (1 - pair) + 1)[i]
            head = (1 - side, 0, 1)[i]
            send(pack1.at[head, :, lanes], in1.at[mine1, lanes], send_in.at[16 + 3 * part + i],
                 recv_in.at[part], other)

    in1[mine1] = pack1[side]
    for head in range(HEADS):
        @pl.when(place == WORKER3[head])
        def _(head=head):
            in3[me] = pack3[head]

    @pl.when(is2)
    def _():
        work[mine2] = pack2[head2]

    def unit_refs(unit):
        head = lax.div(unit, 2)
        segment = lax.rem(unit, 2)
        return head, segment, pl.ds(pl.multiple_of(DIM * head, DIM), DIM)

    def forward0(unit, carry):
        head, segment, lanes = unit_refs(unit)
        rows = pl.ds(pl.multiple_of(KEYS * segment, KEYS), KEYS)
        key, value = keys[rows, lanes], values[rows, lanes]
        for chunk in range(2):
            start = pl.multiple_of(KEYS * segment + 256 * chunk, 256)
            part = pl.ds(start, 256)
            scores = nt(key, query[part, lanes]) * FACTOR
            row_max = jnp.max(scores, 0, keepdims=True)
            powers = jnp.exp(scores - row_max)
            powers0[unit, :, 256 * chunk : 256 * chunk + 256] = powers
            weighted0[head, :, part] = tn(value, powers.astype(BF16))
            stat0[head, 0:1, part] = row_max
            stat0[head, 1:2, part] = jnp.sum(powers, 0, keepdims=True)
        return carry

    lax.fori_loop(0, 4, forward0, 0)
    for head in range(HEADS):
        dout_t[head] = dout[:, DIM * head : DIM * head + DIM].astype(F32).T

    for head in range(HEADS):
        off = [offsets[head, level] for level in range(3)]
        column = iota((1, 256), 1)
        target = jnp.where(
            column < 128,
            column * RATES[0] + off[0],
            jnp.where(
                column < 160, (column - 128) * RATES[1] + off[1], (column - 160) * RATES[2] + off[2]
            ),
        )
        spread[head] = jnp.where(iota((TOKENS, 256), 0) == target, 1.0, 0.0).astype(BF16)
        row = iota((128, 1), 0)
        for ref, level in ((sel2, 1), (sel3, 2)):
            target = (row - bases[level]) * RATES[level] + off[level]
            ref[head] = jnp.where(iota((128, TOKENS), 1) == target, 1.0, 0.0).astype(BF16)

    def item_forward(ref, rows, powers_ref):
        scores = nt(ref[:, 0:128], ref[rows, 256:384]) * FACTOR
        row_max = jnp.max(scores, 0, keepdims=True)
        powers = jnp.exp(scores - row_max)
        powers_ref[...] = powers
        total = jnp.sum(powers, 0, keepdims=True)
        stats = jnp.concatenate([row_max, total, jnp.zeros((6, total.shape[1]), F32)], 0)
        return tn(powers.astype(BF16), ref[:, 128:256]), stats

    def item_backward(ref, rows, powers_ref, log_all, delta_all, row_max, log_own, delta_own):
        k_all, v_all, q_all, d_all = (ref[:, 128 * i : 128 * i + 128] for i in range(4))
        k_own, v_own, d_own = ref[rows, 0:128], ref[rows, 128:256], ref[rows, 384:512]
        probs = powers_ref[...] * jnp.exp(row_max - log_own)
        low = (probs * (nt(v_all, d_own) - delta_own)).astype(BF16)
        grad_q = FACTOR * tn(low, k_all)
        probs = jnp.exp(nt(k_own, q_all) * FACTOR - log_all)
        low = (probs * (nt(v_own, d_all) - delta_all)).astype(BF16)
        grad_k = FACTOR * nn(low, q_all)
        grad_v = nn(probs.astype(BF16), d_all)
        return jnp.concatenate([grad_q, grad_k, grad_v], 1)

    rows1 = pl.ds(pl.multiple_of(256 * pair, 256), 256)
    rows2 = pl.ds(pl.multiple_of(256 * half, 256), 256)
    rows3 = pl.ds(pl.multiple_of(128 * x, 128), 128)
    power3 = power_work.at[:, 0:128]

    @pl.when(is2)
    def _():
        arrived(work.at[pl.ds(0, 480), pl.ds(0, 384)], recv_in.at[2])
        weighted, stats = item_forward(work, rows2, power_work)
        stat_own[:, 0:256] = stats
        for i in range(8):
            tile = stats[:, 128 * (i // 4) : 128 * (i // 4) + 128]
            send2[i] = jnp.concatenate([weighted[32 * i : 32 * i + 32], tile], 0)

    @pl.when(is3)
    def _():
        arrived(in3.at[pl.ds(0, 63)], recv_in.at[4])
        both = in3[...].astype(F32)
        work[:, 0:256] = both[:, 0:8].reshape(KEYS, 256).astype(BF16)
        work[:, 256:512] = both[:, 8:16].reshape(KEYS, 256).astype(BF16)
        weighted, stats = item_forward(work, rows3, power3)
        stat_own[:, 0:128] = stats
        for i in range(16):
            send3[i] = jnp.concatenate([weighted[8 * i : 8 * i + 8], stats], 0)

    def returns(src2, dst2, src3, dst3, sems, recv, wait):
        def each(src, dst, sem, recv_sem, device):
            copy = remote(src, dst, sem, recv_sem, device)
            if wait:
                copy.wait_send()
            else:
                copy.start()

        @pl.when(is2)
        def _():
            here = place - 8 * half

            def step(i, carry):
                other = lax.rem(here + i, 8)
                each(src2.at[other], dst2.at[head2], sems.at[i], recv.at[head2], plane + 8 * half + other)
                return carry

            lax.fori_loop(1, 8, step, 0)
            if not wait:
                dst2[head2] = src2[here]

        @pl.when(is3)
        def _():
            def step(i, carry):
                other = lax.rem(place + i, 16)
                each(src3.at[other], dst3.at[head3], sems.at[i], recv.at[2 + head3], plane + other)
                return carry

            lax.fori_loop(1, 16, step, 0)
            if not wait:
                dst3[head3] = src3[place]

    def returned(dst1, dst2, dst3, recv):
        arrived(dst1.at[1 - side], recv.at[4])
        for head in range(HEADS):
            @pl.when(place != worker2(half, head))
            def _(head=head):
                arrived(dst2.at[head], recv.at[head])

            @pl.when(place != WORKER3[head])
            def _(head=head):
                arrived(dst3.at[head], recv.at[2 + head])

    returns(send2, back2, send3, back3, send_back, recv_back, False)

    arrived(in1.at[pl.ds(0, 448), pl.ds(0, 256)], recv_in.at[0])
    weighted, stats = item_forward(in1, rows1, power1)
    stat1[...] = stats
    for i in range(2):
        send1[i] = jnp.concatenate(
            [weighted[128 * i : 128 * i + 128], stats[:, 128 * i : 128 * i + 128]], 0
        )
    send(send1.at[1 - side], back1.at[side], send_back.at[16], recv_back.at[4], partner)
    back1[side] = send1[side]

    returned(back1, back2, back3, recv_back)
    position = iota((1, TOKENS), 1)
    for head in range(HEADS):
        found = (
            select_rows(back1[head, 128:136], sel[head, 0:128]),
            select_rows(back2[head, 32:40], sel2[head]),
            select_rows(back3[head, 8:16], sel3[head]),
        )
        maxima = [stat0[head, 0:1]]
        for level in range(3):
            member = lax.rem(position, RATES[level]) == offsets[head, level]
            maxima.append(jnp.where(member, found[level][0:1], -jnp.inf))
        peak = jnp.maximum(jnp.maximum(maxima[0], maxima[1]), jnp.maximum(maxima[2], maxima[3]))
        factors = [jnp.exp(item - peak) for item in maxima]
        denominator = factors[0] * stat0[head, 1:2]
        for level in range(3):
            denominator += factors[level + 1] * found[level][1:2]
        log_total = peak + jnp.log(denominator)
        shares = [item / denominator for item in factors]
        lane_shares = select_rows_nt(
            jnp.concatenate(shares[1:] + [jnp.zeros((5, TOKENS), F32)], 0), sel[head]
        )
        lane = iota((1, 256), 1)
        share = jnp.where(lane < 128, lane_shares[0:1], jnp.where(lane < 160, lane_shares[1:2], lane_shares[2:3]))
        stacked = jnp.concatenate(
            [back1[head, 0:128], back2[head, 0:32], back3[head, 0:8], jnp.zeros((88, DIM), F32)], 0
        ).T * share
        high = stacked.astype(BF16)
        low = (stacked - high.astype(F32)).astype(BF16)
        attended = shares[0] * weighted0[head] + nn(high, sel[head]) + nn(low, sel[head])
        delta = jnp.sum(dout_t[head] * attended, 0, keepdims=True)
        att_out[:, DIM * head : DIM * head + DIM] = attended.T
        rows = jnp.concatenate([log_total, delta, jnp.zeros((6, TOKENS), F32)], 0)
        logs[head] = rows
        tiles[0, 2 * head : 2 * head + 2] = select_rows_nt(rows, sel[head, 0:128])[0:2]
        tiles[1, 2 * head : 2 * head + 2] = select_rows_nt(rows, sel2[head])[0:2]
        tiles[2, 2 * head : 2 * head + 2] = select_rows_nt(rows, sel3[head])[0:2]
    for level in range(3):
        tiles[level, 4:8] = jnp.zeros((4, BLOCK), F32)

    for block in range(4):
        for head in range(HEADS):
            send(tiles.at[2], tiles3.at[me], send_stat.at[2 * block + head], recv_stat.at[2],
                 16 * block + WORKER3[head])
    for i in range(4):
        send(tiles.at[1], tiles2.at[place], send_stat.at[8 + i], recv_stat.at[1],
             plane + worker2(i // 2, i % 2))
    for i in range(1, 4):
        send(tiles.at[0], tiles1.at[y], send_stat.at[11 + i], recv_stat.at[0], group + lax.rem(y + i, 4))
    tiles1[y] = tiles[0]

    @pl.when(is2)
    def _():
        tiles2[place] = tiles[1]

    @pl.when(is3)
    def _():
        tiles3[me] = tiles[2]

    def backward0(unit, carry):
        head, segment, lanes = unit_refs(unit)
        rows = pl.ds(pl.multiple_of(KEYS * segment, KEYS), KEYS)
        key, value = keys[rows, lanes], values[rows, lanes]
        grad_k = jnp.zeros((KEYS, DIM), F32)
        grad_v = jnp.zeros((KEYS, DIM), F32)
        for chunk in range(2):
            part = pl.ds(pl.multiple_of(KEYS * segment + 256 * chunk, 256), 256)
            rescale = jnp.exp(stat0[head, 0:1, part] - logs[head, 0:1, part])
            probs = powers0[unit, :, 256 * chunk : 256 * chunk + 256] * rescale
            grad_rows = dout[part, lanes]
            low = (probs * (nt(value, grad_rows) - logs[head, 1:2, part])).astype(BF16)
            grad_k += nn(low, query[part, lanes])
            grad_v += nn(probs.astype(BF16), grad_rows)
            dq_out[part, lanes] = (FACTOR * tn(key, low)).T
        dk_out[rows, lanes] = FACTOR * grad_k
        dv_out[rows, lanes] = grad_v
        return carry

    lax.fori_loop(0, 4, backward0, 0)

    def row_blocks(blocks, head):
        first = head == 0
        return (
            [jnp.where(first, tile[0:1], tile[2:3]) for tile in blocks],
            [jnp.where(first, tile[1:2], tile[3:4]) for tile in blocks],
        )

    def pick(rows, block):
        chosen = rows[0]
        for i in range(1, len(rows)):
            chosen = jnp.where(block == i, rows[i], chosen)
        return chosen

    def pairs(rows):
        return [jnp.concatenate(rows[0:2], 1), jnp.concatenate(rows[2:4], 1)]

    @pl.when(is2)
    def _():
        arrived(work.at[pl.ds(0, 480), pl.ds(0, 128)], recv_in.at[3])
        arrived(tiles2.at[pl.ds(0, 15)], recv_stat.at[1])
        blocks = [jnp.sum(tiles2[4 * i : 4 * i + 4], 0) for i in range(4)]
        log_rows, delta_rows = row_blocks(blocks, head2)
        grads = item_backward(
            work, rows2, power_work, jnp.concatenate(log_rows, 1), jnp.concatenate(delta_rows, 1),
            stat_own[0:1], pick(pairs(log_rows), half), pick(pairs(delta_rows), half),
        ).astype(BF16)
        for i in range(8):
            grad_send2[i] = grads[32 * i : 32 * i + 32]

    @pl.when(is3)
    def _():
        arrived(tiles3.at[pl.ds(0, 63)], recv_stat.at[2])
        blocks = [jnp.sum(tiles3[16 * i : 16 * i + 16], 0) for i in range(4)]
        log_rows, delta_rows = row_blocks(blocks, head3)
        grads = item_backward(
            work, rows3, power3, jnp.concatenate(log_rows, 1), jnp.concatenate(delta_rows, 1),
            stat_own[0:1, 0:128], pick(log_rows, x), pick(delta_rows, x),
        )
        for i in range(16):
            tile = jnp.concatenate([grads[8 * i : 8 * i + 8], jnp.zeros((8, 3 * DIM), F32)], 0)
            grad_send3[i] = tile.astype(BF16)

    stack1 = stack.at[:, 0:128]
    stack2 = stack.at[:, 128:160]
    stack3 = stack.at[:, 160:176]
    returns(grad_send2, stack2, grad_send3, stack3, send_grad, recv_grad, False)

    arrived(in1.at[pl.ds(0, 320), pl.ds(0, 256)], recv_in.at[1])
    arrived(tiles1.at[pl.ds(0, 3)], recv_stat.at[0])
    log_rows, delta_rows = row_blocks([tiles1[i] for i in range(4)], side)
    grads = item_backward(
        in1, rows1, power1, jnp.concatenate(log_rows, 1), jnp.concatenate(delta_rows, 1),
        stat1[0:1], pick(pairs(log_rows), pair), pick(pairs(delta_rows), pair),
    ).astype(BF16)
    for i in range(2):
        grad_send1[i] = grads[128 * i : 128 * i + 128]
    send(grad_send1.at[1 - side], stack1.at[side], send_grad.at[16], recv_grad.at[4], partner)
    stack1[side] = grad_send1[side]

    stack_out[:, 176:256] = jnp.zeros((2, 80, 3 * DIM), BF16)
    returned(stack1, stack2, stack3, recv_grad)
    stack_out[:, 0:176] = stack[...]

    for device, copy in pending:
        @pl.when(device != me)
        def _(copy=copy):
            copy.wait_send()
    returns(send2, back2, send3, back3, send_back, recv_back, True)
    returns(grad_send2, stack2, grad_send3, stack3, send_grad, recv_grad, True)


def finish(att, dq, dk, dv, spread, stack, att_out, dq_out, dk_out, dv_out, full, sems):
    first = pltpu.make_async_copy(att, att_out, sems.at[12])
    first.start()
    copies = [first]
    for part in range(4):
        rows = slice(256 * part, 256 * part + 256)
        for head in range(HEADS):
            lanes = slice(DIM * head, DIM * head + DIM)
            added = nn(spread[head, rows], stack[head])
            for i, ref in enumerate((dq, dk, dv)):
                full[i, rows, lanes] = ref[rows, lanes] + added[:, DIM * i : DIM * i + DIM]
        for i, out in enumerate((dq_out, dk_out, dv_out)):
            copies.append(
                pltpu.make_async_copy(full.at[i, rows], out.at[rows], sems.at[3 * part + i])
            )
            copies[-1].start()
    for copy in copies:
        copy.wait()


def body(query, keys, values, grad_out, offsets):
    vmem = pl.BlockSpec(memory_space=pltpu.VMEM)
    hbm = pl.BlockSpec(memory_space=pltpu.HBM)
    smem = pl.BlockSpec(memory_space=pltpu.SMEM)
    out = jax.ShapeDtypeStruct((TOKENS, HEADS * DIM), F32)
    dma = pltpu.SemaphoreType.DMA
    held = pltpu.VMEM((TOKENS, HEADS * DIM), BF16)
    parts = pl.pallas_call(
        kernel,
        out_shape=(
            out, out, out, out,
            jax.ShapeDtypeStruct((2, TOKENS, 256), BF16),
            jax.ShapeDtypeStruct((2, 256, 3 * DIM), BF16),
        ),
        in_specs=[smem, hbm, hbm, hbm, hbm],
        out_specs=(vmem,) * 6,
        scratch_shapes=[
            held, held, held, held,
            pltpu.VMEM((2, 256, TOKENS), BF16),
            pltpu.VMEM((2, 128, TOKENS), BF16),
            pltpu.VMEM((2, 128, TOKENS), BF16),
            pltpu.VMEM((2, DIM, TOKENS), F32),
            pltpu.VMEM((4, KEYS, KEYS), F32),
            pltpu.VMEM((2, DIM, TOKENS), F32),
            pltpu.VMEM((2, 8, TOKENS), F32),
            pltpu.VMEM((2, 8, TOKENS), F32),
            pltpu.VMEM((2, 128, 512), BF16),
            pltpu.VMEM((2, 32, 512), BF16),
            pltpu.VMEM((2, 16, 256), BF16),
            pltpu.VMEM((512, 512), BF16),
            pltpu.VMEM((512, 512), BF16),
            pltpu.VMEM((64, 16, 256), BF16),
            pltpu.VMEM((512, 256), F32),
            pltpu.VMEM((512, 256), F32),
            pltpu.VMEM((8, 256), F32),
            pltpu.VMEM((8, 256), F32),
            pltpu.VMEM((2, 136, 128), F32),
            pltpu.VMEM((8, 40, 128), F32),
            pltpu.VMEM((16, 16, 128), F32),
            pltpu.VMEM((2, 136, 128), F32),
            pltpu.VMEM((2, 40, 128), F32),
            pltpu.VMEM((2, 16, 128), F32),
            pltpu.VMEM((2, 128, 384), BF16),
            pltpu.VMEM((8, 32, 384), BF16),
            pltpu.VMEM((16, 16, 384), BF16),
            pltpu.VMEM((2, 176, 384), BF16),
            pltpu.VMEM((3, 8, 128), F32),
            pltpu.VMEM((4, 8, 128), F32),
            pltpu.VMEM((16, 8, 128), F32),
            pltpu.VMEM((64, 8, 128), F32),
            dma((4,)),
            dma((22,)),
            dma((17,)),
            dma((15,)),
            dma((17,)),
            dma((5,)),
            dma((5,)),
            dma((3,)),
            dma((5,)),
        ],
        compiler_params=pltpu.CompilerParams(
            collective_id=0, has_side_effects=True, vmem_limit_bytes=32 * 2**20
        ),
    )(offsets.T, query, keys, values, grad_out)
    return pl.pallas_call(
        finish,
        out_shape=(out, out, out, out),
        in_specs=[vmem] * 6,
        out_specs=(hbm,) * 4,
        scratch_shapes=[pltpu.VMEM((3, TOKENS, HEADS * DIM), F32), dma((13,))],
        compiler_params=pltpu.CompilerParams(vmem_limit_bytes=16 * 2**20),
    )(*parts)


def solution(mesh):
    spec = P("seq", "rep")
    return jax.shard_map(
        body,
        mesh=mesh,
        in_specs=(spec, spec, spec, spec, P(None, "rep")),
        out_specs=(spec, spec, spec, spec),
        check_vma=False,
    )
```

time: 53.3 us -> 45.2 us (0.85)
  local copies, waits for them, and re-layouts: 9.44 us -> 4.84 us
  Pallas kernels: 42.9 us -> 39.4 us
    unnamed x15 -> x10, local copies, waits for them, and re-layouts: 9.44 us -> 4.84 us
    pallas_call x1 -> x2, Pallas kernels: 42.9 us -> 39.4 us  [the longest x1 37.3 us: body(): pl.pallas_call(kernel, out_shape=(out, out, out, out, jax.ShapeDtypeStruc...]
where the time goes in v2:
time: 45.2 us; the launch traced here: 44.9 us
  Pallas kernels  39.4 us (87%)
  local copies, waits for them, and re-layouts  4.84 us (11%)
  between operations  0.65 us (1%)
    pallas_call x1, Pallas kernels, body(): pl.pallas_call(kernel, out_shape=(out, out, out, out, jax.ShapeDtypeStruc...  37.3 us
    unnamed x10, local copies, waits for them, and re-layouts  4.84 us
    pallas_call x1, Pallas kernels, body(): pl.pallas_call(finish, out_shape=(out, out, out, out), in_specs=[vmem] *...  2.13 us

profile of v2, /device:TPU:8, one launch (start us, length us, event | category | flops | bytes accessed | tf_op | source)
XLA Modules:
  0.0 44.9 jit_solution(2912423891021031210)
XLA Ops:
  0.6 0.0 copy-start.4
  0.6 0.7 %copy-done.4 = s32[3,2]{0,1:T(2,128)S(1)} copy-done((s32[3,2]{0,1:T(2,128)S(1)}, s32[3,2]{0,1:T(2,128)}, u32[]{:S(2)}) %copy-start.4) | copy-done | bytes 48
  1.3 0.0 copy-start
  1.3 1.0 %copy-done = bf16[1024,256]{1,0:T(8,128)(2,1)S(1)} copy-done((bf16[1024,256]{1,0:T(8,128)(2,1)S(1)}, bf16[1024,256]{1,0:T(8,128)(2,1)}, u32[]{:S(2)}) %copy-start) | copy-done | bytes 524312
  2.4 0.0 copy-start.1
  2.4 1.0 %copy-done.1 = bf16[1024,256]{1,0:T(8,128)(2,1)S(1)} copy-done((bf16[1024,256]{1,0:T(8,128)(2,1)S(1)}, bf16[1024,256]{1,0:T(8,128)(2,1)}, u32[]{:S(2)}) %copy-start.1) | copy-done | bytes 524312
  3.4 0.0 copy-start.2
  3.4 1.0 %copy-done.2 = bf16[1024,256]{1,0:T(8,128)(2,1)S(1)} copy-done((bf16[1024,256]{1,0:T(8,128)(2,1)S(1)}, bf16[1024,256]{1,0:T(8,128)(2,1)}, u32[]{:S(2)}) %copy-start.2) | copy-done | bytes 524312
  4.4 0.0 copy-start.3
  4.4 1.0 %copy-done.3 = bf16[1024,256]{1,0:T(8,128)(2,1)S(1)} copy-done((bf16[1024,256]{1,0:T(8,128)(2,1)S(1)}, bf16[1024,256]{1,0:T(8,128)(2,1)}, u32[]{:S(2)}) %copy-start.3) | copy-done | bytes 524312
  5.5 37.3 %shard_map.84 = (f32[1024,256]{1,0:T(8,128)S(1)}, f32[1024,256]{1,0:T(8,128)S(1)}, f32[1024,256]{1,0:T(8,128)S(1)}, f32[1024,256]{1,0:T(8,128)S(1)}, bf16[2,1024...) custom-call(s32[2,3]{1,0:T(2,128)S(1)} %bitcast.1, bf16[1024,256]{1,0:T(8,128)(2,1)S(1)} %copy-done, ...), custom_call_target="tpu_custom_call" | custom-call | tf_op jit(solution)/shard_map/pallas_call | solution.py:537
  42.8 2.1 %shard_map.85 = (f32[1024,256]{1,0:T(8,128)}, f32[1024,256]{1,0:T(8,128)}, f32[1024,256]{1,0:T(8,128)}, f32[1024,256]{1,0:T(8,128)}) custom-call(f32[1024,256]{1,0:T(8,128)S(1)} %get-tuple-element.10.att, f32[1024,256]{1,0:T(8,128)S(1)} %get-tuple-element.11.dq, f32[1024,256]{1,0:T(8,128)S(1)} %get-tuple-element.12.dk, ...), custom_call_target="tpu_custom_call" | custom-call | tf_op jit(solution)/shard_map/pallas_call | solution.py:594
Async XLA Ops:
  0.6 0.7 %copy-start.4 = (s32[3,2]{0,1:T(2,128)S(1)}, s32[3,2]{0,1:T(2,128)}, u32[]{:S(2)}) copy-start(s32[3,2]{0,1:T(2,128)} %param.9) | copy-start | bytes 76
  1.3 1.0 %copy-start = (bf16[1024,256]{1,0:T(8,128)(2,1)S(1)}, bf16[1024,256]{1,0:T(8,128)(2,1)}, u32[]{:S(2)}) copy-start(bf16[1024,256]{1,0:T(8,128)(2,1)} %query_hbm.1) | copy-start | bytes 1572868
  2.4 1.0 %copy-start.1 = (bf16[1024,256]{1,0:T(8,128)(2,1)S(1)}, bf16[1024,256]{1,0:T(8,128)(2,1)}, u32[]{:S(2)}) copy-start(bf16[1024,256]{1,0:T(8,128)(2,1)} %keys_hbm.1) | copy-start | bytes 1572868
  3.4 1.0 %copy-start.2 = (bf16[1024,256]{1,0:T(8,128)(2,1)S(1)}, bf16[1024,256]{1,0:T(8,128)(2,1)}, u32[]{:S(2)}) copy-start(bf16[1024,256]{1,0:T(8,128)(2,1)} %values_hbm.1) | copy-start | bytes 1572868
  4.4 1.0 %copy-start.3 = (bf16[1024,256]{1,0:T(8,128)(2,1)S(1)}, bf16[1024,256]{1,0:T(8,128)(2,1)}, u32[]{:S(2)}) copy-start(bf16[1024,256]{1,0:T(8,128)(2,1)} %dout_hbm.1) | copy-start | bytes 1572868

commit v3 on v2

--- a/solution.py
+++ b/solution.py
@@ -65,11 +65,11 @@
 
 
 def kernel(
-    offsets, query_hbm, keys_hbm, values_hbm, dout_hbm,
+    offsets_hbm, query_hbm, keys_hbm, values_hbm, dout_hbm,
     att_out, dq_out, dk_out, dv_out, spread, stack_out,
-    query, keys, values, dout,
-    sel, sel2, sel3, dout_t, powers0, weighted0, stat0, logs,
-    pack1, pack2, pack3, in1, work, in3, power1, power_work, stat1, stat_own,
+    offsets, query, keys, values, dout,
+    sel, sel2, sel3, powers0, products0, shares, weighted0, stat0, logs,
+    pack1, pack2, pack3, in1, work, in3, power1, power_work, product1, product_work, stat1, stat_own,
     send1, send2, send3, back1, back2, back3, grad_send1, grad_send2, grad_send3, stack,
     tiles, tiles1, tiles2, tiles3,
     load_sem, send_in, send_back, send_stat, send_grad,
@@ -93,6 +93,8 @@
     one2 = jnp.where(is2, 1, 0)
     one3 = jnp.where(is3, 1, 0)
 
+    load_offsets = pltpu.make_async_copy(offsets_hbm, offsets, load_sem.at[4])
+    load_offsets.start()
     loads = []
     for i, (source, held) in enumerate(
         ((query_hbm, query), (keys_hbm, keys), (values_hbm, values), (dout_hbm, dout))
@@ -136,6 +138,7 @@
         greet(group + lax.rem(y + i, 4))
 
     bases = (0, 32 * y, 8 * place)
+    load_offsets.wait()
     for head in range(HEADS):
         off = [offsets[head, level] for level in range(3)]
 
@@ -191,18 +194,18 @@
         for head in range(HEADS):
             send(pack3.at[head], in3.at[me], send_in.at[2 * block + head], recv_in.at[4],
                  16 * block + WORKER3[head])
+    for head in range(HEADS):
+        send(pack2.at[head], work.at[mine2], send_in.at[8 + head], recv_in.at[2],
+             plane + worker2(half, head))
+    send(pack1.at[1 - side], in1.at[mine1], send_in.at[10], recv_in.at[0], partner)
+    other_pair = group + 2 * (1 - pair)
     for part in range(2):
-        for i in range(4):
-            lanes = (slice(0, 384), slice(384, 512))[part]
-            send(pack2.at[i % 2, :, lanes], work.at[mine2, lanes], send_in.at[8 + 4 * part + i],
-                 recv_in.at[2 + part], plane + worker2(i // 2, i % 2))
-        for i in range(3):
-            wide = 384 if i == 0 else 256
-            lanes = (slice(0, wide), slice(wide, 512))[part]
-            other = (partner, group + 2 * (1 - pair), group + 2 * (1 - pair) + 1)[i]
-            head = (1 - side, 0, 1)[i]
-            send(pack1.at[head, :, lanes], in1.at[mine1, lanes], send_in.at[16 + 3 * part + i],
-                 recv_in.at[part], other)
+        lanes = (slice(0, 256), slice(256, 512))[part]
+        for head in range(HEADS):
+            send(pack2.at[head, :, lanes], work.at[mine2, lanes], send_in.at[11 + 4 * part + head],
+                 recv_in.at[2 + part], plane + worker2(1 - half, head))
+            send(pack1.at[head, :, lanes], in1.at[mine1, lanes], send_in.at[13 + 4 * part + head],
+                 recv_in.at[part], other_pair + head)
 
     in1[mine1] = pack1[side]
     for head in range(HEADS):
@@ -230,15 +233,16 @@
             row_max = jnp.max(scores, 0, keepdims=True)
             powers = jnp.exp(scores - row_max)
             powers0[unit, :, 256 * chunk : 256 * chunk + 256] = powers
-            weighted0[head, :, part] = tn(value, powers.astype(BF16))
+            weights = powers.astype(BF16)
+            weighted0[head, :, part] = tn(value, weights)
+            products = nt(value, dout[part, lanes])
+            products0[unit, :, 256 * chunk : 256 * chunk + 256] = products
             stat0[head, 0:1, part] = row_max
             stat0[head, 1:2, part] = jnp.sum(powers, 0, keepdims=True)
+            stat0[head, 2:3, part] = jnp.sum(weights.astype(F32) * products, 0, keepdims=True)
         return carry
 
     lax.fori_loop(0, 4, forward0, 0)
-    for head in range(HEADS):
-        dout_t[head] = dout[:, DIM * head : DIM * head + DIM].astype(F32).T
-
     for head in range(HEADS):
         off = [offsets[head, level] for level in range(3)]
         column = iota((1, 256), 1)
@@ -255,20 +259,32 @@
             target = (row - bases[level]) * RATES[level] + off[level]
             ref[head] = jnp.where(iota((128, TOKENS), 1) == target, 1.0, 0.0).astype(BF16)
 
-    def item_forward(ref, rows, powers_ref):
+    def item_forward(ref, rows, powers_ref, products_ref):
         scores = nt(ref[:, 0:128], ref[rows, 256:384]) * FACTOR
         row_max = jnp.max(scores, 0, keepdims=True)
         powers = jnp.exp(scores - row_max)
         powers_ref[...] = powers
-        total = jnp.sum(powers, 0, keepdims=True)
-        stats = jnp.concatenate([row_max, total, jnp.zeros((6, total.shape[1]), F32)], 0)
-        return tn(powers.astype(BF16), ref[:, 128:256]), stats
-
-    def item_backward(ref, rows, powers_ref, log_all, delta_all, row_max, log_own, delta_own):
-        k_all, v_all, q_all, d_all = (ref[:, 128 * i : 128 * i + 128] for i in range(4))
-        k_own, v_own, d_own = ref[rows, 0:128], ref[rows, 128:256], ref[rows, 384:512]
+        weights = powers.astype(BF16)
+        products = nt(ref[:, 128:256], ref[rows, 384:512])
+        products_ref[...] = products
+        stats = jnp.concatenate(
+            [
+                row_max,
+                jnp.sum(powers, 0, keepdims=True),
+                jnp.sum(weights.astype(F32) * products, 0, keepdims=True),
+                jnp.zeros((5, row_max.shape[1]), F32),
+            ],
+            0,
+        )
+        return tn(weights, ref[:, 128:256]), stats
+
+    def item_backward(
+        ref, rows, powers_ref, products_ref, log_all, delta_all, row_max, log_own, delta_own
+    ):
+        k_all, q_all, d_all = ref[:, 0:128], ref[:, 256:384], ref[:, 384:512]
+        k_own, v_own = ref[rows, 0:128], ref[rows, 128:256]
         probs = powers_ref[...] * jnp.exp(row_max - log_own)
-        low = (probs * (nt(v_all, d_own) - delta_own)).astype(BF16)
+        low = (probs * (products_ref[...] - delta_own)).astype(BF16)
         grad_q = FACTOR * tn(low, k_all)
         probs = jnp.exp(nt(k_own, q_all) * FACTOR - log_all)
         low = (probs * (nt(v_own, d_all) - delta_all)).astype(BF16)
@@ -280,11 +296,12 @@
     rows2 = pl.ds(pl.multiple_of(256 * half, 256), 256)
     rows3 = pl.ds(pl.multiple_of(128 * x, 128), 128)
     power3 = power_work.at[:, 0:128]
+    product3 = product_work.at[:, 0:128]
 
     @pl.when(is2)
     def _():
-        arrived(work.at[pl.ds(0, 480), pl.ds(0, 384)], recv_in.at[2])
-        weighted, stats = item_forward(work, rows2, power_work)
+        arrived(work.at[pl.ds(0, 352)], recv_in.at[2])
+        weighted, stats = item_forward(work, rows2, power_work, product_work)
         stat_own[:, 0:256] = stats
         for i in range(8):
             tile = stats[:, 128 * (i // 4) : 128 * (i // 4) + 128]
@@ -296,7 +313,7 @@
         both = in3[...].astype(F32)
         work[:, 0:256] = both[:, 0:8].reshape(KEYS, 256).astype(BF16)
         work[:, 256:512] = both[:, 8:16].reshape(KEYS, 256).astype(BF16)
-        weighted, stats = item_forward(work, rows3, power3)
+        weighted, stats = item_forward(work, rows3, power3, product3)
         stat_own[:, 0:128] = stats
         for i in range(16):
             send3[i] = jnp.concatenate([weighted[8 * i : 8 * i + 8], stats], 0)
@@ -346,8 +363,8 @@
 
     returns(send2, back2, send3, back3, send_back, recv_back, False)
 
-    arrived(in1.at[pl.ds(0, 448), pl.ds(0, 256)], recv_in.at[0])
-    weighted, stats = item_forward(in1, rows1, power1)
+    arrived(in1.at[:, pl.ds(0, 256)], recv_in.at[0])
+    weighted, stats = item_forward(in1, rows1, power1, product1)
     stat1[...] = stats
     for i in range(2):
         send1[i] = jnp.concatenate(
@@ -373,26 +390,18 @@
         denominator = factors[0] * stat0[head, 1:2]
         for level in range(3):
             denominator += factors[level + 1] * found[level][1:2]
+        product = factors[0] * stat0[head, 2:3]
+        for level in range(3):
+            product += factors[level + 1] * found[level][2:3]
         log_total = peak + jnp.log(denominator)
-        shares = [item / denominator for item in factors]
-        lane_shares = select_rows_nt(
-            jnp.concatenate(shares[1:] + [jnp.zeros((5, TOKENS), F32)], 0), sel[head]
-        )
-        lane = iota((1, 256), 1)
-        share = jnp.where(lane < 128, lane_shares[0:1], jnp.where(lane < 160, lane_shares[1:2], lane_shares[2:3]))
-        stacked = jnp.concatenate(
-            [back1[head, 0:128], back2[head, 0:32], back3[head, 0:8], jnp.zeros((88, DIM), F32)], 0
-        ).T * share
-        high = stacked.astype(BF16)
-        low = (stacked - high.astype(F32)).astype(BF16)
-        attended = shares[0] * weighted0[head] + nn(high, sel[head]) + nn(low, sel[head])
-        delta = jnp.sum(dout_t[head] * attended, 0, keepdims=True)
-        att_out[:, DIM * head : DIM * head + DIM] = attended.T
-        rows = jnp.concatenate([log_total, delta, jnp.zeros((6, TOKENS), F32)], 0)
+        inverse = 1.0 / denominator
+        rows = jnp.concatenate([log_total, product * inverse, jnp.zeros((6, TOKENS), F32)], 0)
         logs[head] = rows
-        tiles[0, 2 * head : 2 * head + 2] = select_rows_nt(rows, sel[head, 0:128])[0:2]
-        tiles[1, 2 * head : 2 * head + 2] = select_rows_nt(rows, sel2[head])[0:2]
-        tiles[2, 2 * head : 2 * head + 2] = select_rows_nt(rows, sel3[head])[0:2]
+        shares[head] = jnp.concatenate(
+            [item * inverse for item in factors] + [jnp.zeros((4, TOKENS), F32)], 0
+        )
+        for level, chooser in enumerate((sel[head, 0:128], sel2[head], sel3[head])):
+            tiles[level, 2 * head : 2 * head + 2] = select_rows_nt(rows, chooser)[0:2]
     for level in range(3):
         tiles[level, 4:8] = jnp.zeros((4, BLOCK), F32)
 
@@ -418,7 +427,7 @@
     def backward0(unit, carry):
         head, segment, lanes = unit_refs(unit)
         rows = pl.ds(pl.multiple_of(KEYS * segment, KEYS), KEYS)
-        key, value = keys[rows, lanes], values[rows, lanes]
+        key = keys[rows, lanes]
         grad_k = jnp.zeros((KEYS, DIM), F32)
         grad_v = jnp.zeros((KEYS, DIM), F32)
         for chunk in range(2):
@@ -426,7 +435,8 @@
             rescale = jnp.exp(stat0[head, 0:1, part] - logs[head, 0:1, part])
             probs = powers0[unit, :, 256 * chunk : 256 * chunk + 256] * rescale
             grad_rows = dout[part, lanes]
-            low = (probs * (nt(value, grad_rows) - logs[head, 1:2, part])).astype(BF16)
+            products = products0[unit, :, 256 * chunk : 256 * chunk + 256]
+            low = (probs * (products - logs[head, 1:2, part])).astype(BF16)
             grad_k += nn(low, query[part, lanes])
             grad_v += nn(probs.astype(BF16), grad_rows)
             dq_out[part, lanes] = (FACTOR * tn(key, low)).T
@@ -434,7 +444,7 @@
         dv_out[rows, lanes] = grad_v
         return carry
 
-    lax.fori_loop(0, 4, backward0, 0)
+    lax.fori_loop(0, 3, backward0, 0)
 
     def row_blocks(blocks, head):
         first = head == 0
@@ -454,12 +464,12 @@
 
     @pl.when(is2)
     def _():
-        arrived(work.at[pl.ds(0, 480), pl.ds(0, 128)], recv_in.at[3])
+        arrived(work.at[pl.ds(0, 128)], recv_in.at[3])
         arrived(tiles2.at[pl.ds(0, 15)], recv_stat.at[1])
         blocks = [jnp.sum(tiles2[4 * i : 4 * i + 4], 0) for i in range(4)]
         log_rows, delta_rows = row_blocks(blocks, head2)
         grads = item_backward(
-            work, rows2, power_work, jnp.concatenate(log_rows, 1), jnp.concatenate(delta_rows, 1),
+            work, rows2, power_work, product_work, jnp.concatenate(log_rows, 1), jnp.concatenate(delta_rows, 1),
             stat_own[0:1], pick(pairs(log_rows), half), pick(pairs(delta_rows), half),
         ).astype(BF16)
         for i in range(8):
@@ -471,7 +481,7 @@
         blocks = [jnp.sum(tiles3[16 * i : 16 * i + 16], 0) for i in range(4)]
         log_rows, delta_rows = row_blocks(blocks, head3)
         grads = item_backward(
-            work, rows3, power3, jnp.concatenate(log_rows, 1), jnp.concatenate(delta_rows, 1),
+            work, rows3, power3, product3, jnp.concatenate(log_rows, 1), jnp.concatenate(delta_rows, 1),
             stat_own[0:1, 0:128], pick(log_rows, x), pick(delta_rows, x),
         )
         for i in range(16):
@@ -483,17 +493,33 @@
     stack3 = stack.at[:, 160:176]
     returns(grad_send2, stack2, grad_send3, stack3, send_grad, recv_grad, False)
 
-    arrived(in1.at[pl.ds(0, 320), pl.ds(0, 256)], recv_in.at[1])
+    arrived(in1.at[pl.ds(0, 256), pl.ds(0, 256)], recv_in.at[1])
     arrived(tiles1.at[pl.ds(0, 3)], recv_stat.at[0])
     log_rows, delta_rows = row_blocks([tiles1[i] for i in range(4)], side)
     grads = item_backward(
-        in1, rows1, power1, jnp.concatenate(log_rows, 1), jnp.concatenate(delta_rows, 1),
+        in1, rows1, power1, product1,
+        jnp.concatenate(log_rows, 1), jnp.concatenate(delta_rows, 1),
         stat1[0:1], pick(pairs(log_rows), pair), pick(pairs(delta_rows), pair),
     ).astype(BF16)
     for i in range(2):
         grad_send1[i] = grads[128 * i : 128 * i + 128]
     send(grad_send1.at[1 - side], stack1.at[side], send_grad.at[16], recv_grad.at[4], partner)
     stack1[side] = grad_send1[side]
+
+    lax.fori_loop(3, 4, backward0, 0)
+    for head in range(HEADS):
+        lane_shares = select_rows_nt(shares[head], sel[head])
+        lane = iota((1, 256), 1)
+        share = jnp.where(
+            lane < 128, lane_shares[1:2], jnp.where(lane < 160, lane_shares[2:3], lane_shares[3:4])
+        )
+        stacked = jnp.concatenate(
+            [back1[head, 0:128], back2[head, 0:32], back3[head, 0:8], jnp.zeros((88, DIM), F32)], 0
+        ).T * share
+        high = stacked.astype(BF16)
+        low = (stacked - high.astype(F32)).astype(BF16)
+        attended = shares[head, 0:1] * weighted0[head] + nn(high, sel[head]) + nn(low, sel[head])
+        att_out[:, DIM * head : DIM * head + DIM] = attended.T
 
     stack_out[:, 176:256] = jnp.zeros((2, 80, 3 * DIM), BF16)
     returned(stack1, stack2, stack3, recv_grad)
@@ -530,10 +556,13 @@
 def body(query, keys, values, grad_out, offsets):
     vmem = pl.BlockSpec(memory_space=pltpu.VMEM)
     hbm = pl.BlockSpec(memory_space=pltpu.HBM)
-    smem = pl.BlockSpec(memory_space=pltpu.SMEM)
     out = jax.ShapeDtypeStruct((TOKENS, HEADS * DIM), F32)
     dma = pltpu.SemaphoreType.DMA
     held = pltpu.VMEM((TOKENS, HEADS * DIM), BF16)
+    pinned = [
+        pltpu.with_memory_space_constraint(item, pltpu.HBM)
+        for item in (offsets.T, query, keys, values, grad_out)
+    ]
     parts = pl.pallas_call(
         kernel,
         out_shape=(
@@ -541,15 +570,17 @@
             jax.ShapeDtypeStruct((2, TOKENS, 256), BF16),
             jax.ShapeDtypeStruct((2, 256, 3 * DIM), BF16),
         ),
-        in_specs=[smem, hbm, hbm, hbm, hbm],
+        in_specs=[hbm] * 5,
         out_specs=(vmem,) * 6,
         scratch_shapes=[
+            pltpu.SMEM((HEADS, 3), jnp.int32),
             held, held, held, held,
             pltpu.VMEM((2, 256, TOKENS), BF16),
             pltpu.VMEM((2, 128, TOKENS), BF16),
             pltpu.VMEM((2, 128, TOKENS), BF16),
-            pltpu.VMEM((2, DIM, TOKENS), F32),
             pltpu.VMEM((4, KEYS, KEYS), F32),
+            pltpu.VMEM((4, KEYS, KEYS), F32),
+            pltpu.VMEM((2, 8, TOKENS), F32),
             pltpu.VMEM((2, DIM, TOKENS), F32),
             pltpu.VMEM((2, 8, TOKENS), F32),
             pltpu.VMEM((2, 8, TOKENS), F32),
@@ -559,6 +590,8 @@
             pltpu.VMEM((512, 512), BF16),
             pltpu.VMEM((512, 512), BF16),
             pltpu.VMEM((64, 16, 256), BF16),
+            pltpu.VMEM((512, 256), F32),
+            pltpu.VMEM((512, 256), F32),
             pltpu.VMEM((512, 256), F32),
             pltpu.VMEM((512, 256), F32),
             pltpu.VMEM((8, 256), F32),
@@ -577,8 +610,8 @@
             pltpu.VMEM((4, 8, 128), F32),
             pltpu.VMEM((16, 8, 128), F32),
             pltpu.VMEM((64, 8, 128), F32),
-            dma((4,)),
-            dma((22,)),
+            dma((5,)),
+            dma((19,)),
             dma((17,)),
             dma((15,)),
             dma((17,)),
@@ -590,7 +623,7 @@
         compiler_params=pltpu.CompilerParams(
             collective_id=0, has_side_effects=True, vmem_limit_bytes=32 * 2**20
         ),
-    )(offsets.T, query, keys, values, grad_out)
+    )(*pinned)
     return pl.pallas_call(
         finish,
         out_shape=(out, out, out, out),

time: 45.2 us -> 38.5 us (0.85)
  local copies, waits for them, and re-layouts: 4.84 us -> 0 us
  Pallas kernels: 39.4 us -> 37.7 us
    unnamed x10 -> x0, local copies, waits for them, and re-layouts: 4.84 us -> none
    pallas_call x1, Pallas kernels: 37.3 us -> 35.6 us  [body(): pl.pallas_call(kernel, out_shape=(out, out, out, out, jax.ShapeDtypeStruc...]
where the time goes in v3:
time: 38.5 us; the launch traced here: 38.3 us
  Pallas kernels  37.7 us (98%)
  between operations  0.64 us (2%)
    pallas_call x1, Pallas kernels, body(): pl.pallas_call(kernel, out_shape=(out, out, out, out, jax.ShapeDtypeStruc...  35.6 us
    pallas_call x1, Pallas kernels, body(): pl.pallas_call(finish, out_shape=(out, out, out, out), in_specs=[vmem] *...  2.13 us

profile of v3, /device:TPU:8, one launch (start us, length us, event | category | flops | bytes accessed | tf_op | source)
XLA Modules:
  0.0 38.3 jit_solution(10094756101367138789)
XLA Ops:
  0.6 35.6 %shard_map.84 = (f32[1024,256]{1,0:T(8,128)S(1)}, f32[1024,256]{1,0:T(8,128)S(1)}, f32[1024,256]{1,0:T(8,128)S(1)}, f32[1024,256]{1,0:T(8,128)S(1)}, bf16[2,1024...) custom-call(s32[2,3]{1,0:T(2,128)} %bitcast.1, bf16[1024,256]{1,0:T(8,128)(2,1)} %query_hbm.1, ...), custom_call_target="tpu_custom_call" | custom-call | tf_op jit(solution)/shard_map/pallas_call | solution.py:566
  36.2 2.1 %shard_map.85 = (f32[1024,256]{1,0:T(8,128)}, f32[1024,256]{1,0:T(8,128)}, f32[1024,256]{1,0:T(8,128)}, f32[1024,256]{1,0:T(8,128)}) custom-call(f32[1024,256]{1,0:T(8,128)S(1)} %get-tuple-element.10.att, f32[1024,256]{1,0:T(8,128)S(1)} %get-tuple-element.11.dq, f32[1024,256]{1,0:T(8,128)S(1)} %get-tuple-element.12.dk, ...), custom_call_target="tpu_custom_call" | custom-call | tf_op jit(solution)/shard_map/pallas_call | solution.py:627

commit v4 on v3

--- a/solution.py
+++ b/solution.py
@@ -16,8 +16,6 @@
 F32 = jnp.float32
 BF16 = jnp.bfloat16
 
-WORKER3 = (5, 11)
-
 
 def dot(a, b, dims):
     return lax.dot_general(a, b, (dims, ((), ())), preferred_element_type=F32)
@@ -60,20 +58,16 @@
     return lax.broadcasted_iota(jnp.int32, shape, dim)
 
 
-def worker2(half, head):
-    return 4 * (1 + half) + 2 * head
-
-
 def kernel(
     offsets_hbm, query_hbm, keys_hbm, values_hbm, dout_hbm,
     att_out, dq_out, dk_out, dv_out, spread, stack_out,
     offsets, query, keys, values, dout,
     sel, sel2, sel3, powers0, products0, shares, weighted0, stat0, logs,
-    pack1, pack2, pack3, in1, work, in3, power1, power_work, product1, product_work, stat1, stat_own,
-    send1, send2, send3, back1, back2, back3, grad_send1, grad_send2, grad_send3, stack,
+    pack1, pack2, pack3, work, in3, power_work, product_work, stat_work, weighted_work,
+    stat_send, send2, send3, back_stat1, back_rows1, back2, back3, grad_work, grad_send3, stack,
     tiles, tiles1, tiles2, tiles3,
-    load_sem, send_in, send_back, send_stat, send_grad,
-    recv_in, recv_back, recv_stat, recv_grad,
+    load_sem, send_in, send_back, send_back1, send_rows1, send_stat, send_grad, send_grad1,
+    recv_in, recv_back, recv_back1, recv_rows1, recv_stat, recv_grad, recv_grad1,
 ):
     me = lax.axis_index("seq")
     y = lax.rem(me, 4)
@@ -82,14 +76,15 @@
     place = lax.rem(me, 16)
     plane = me - place
     group = me - y
-    side = lax.rem(y, 2)
-    pair = lax.div(y, 2)
-    partner = group + 2 * pair + 1 - side
-    half = lax.div(z, 2)
-    is2 = (side == 0) & ((z == 1) | (z == 2))
-    head2 = pair
-    is3 = (place == WORKER3[0]) | (place == WORKER3[1])
-    head3 = jnp.where(place == WORKER3[0], 0, 1)
+    core = lax.rem(lax.axis_index("rep"), 2)
+    worker1 = (core, 2 + core)
+    worker2 = (5 + core, 9 + core)
+    worker3 = (7 - 3 * core, 11 - 3 * core)
+    is1 = (y == worker1[0]) | (y == worker1[1])
+    is2 = (place == worker2[0]) | (place == worker2[1])
+    is3 = (place == worker3[0]) | (place == worker3[1])
+    head12 = jnp.where((is1 & (y == worker1[0])) | (is2 & (place == worker2[0])), 0, 1)
+    head3 = jnp.where(place == worker3[0], 0, 1)
     one2 = jnp.where(is2, 1, 0)
     one3 = jnp.where(is3, 1, 0)
 
@@ -123,13 +118,7 @@
 
         lax.fori_loop(1, 16, step, 0)
 
-    for spot in WORKER3:
-        @pl.when(place != spot)
-        def _(spot=spot):
-            greet(plane + spot)
-    for head in range(HEADS):
-        spot = worker2(half, head)
-
+    for spot in worker2 + worker3:
         @pl.when(place != spot)
         def _(spot=spot):
             greet(plane + spot)
@@ -167,7 +156,7 @@
         pack2[head, :, 256:512] = second[128:160].astype(BF16)
         pack3[head] = jnp.concatenate([first[160:168], second[160:168]], 0).astype(BF16)
 
-    pl.semaphore_wait(barrier, 3 + (4 - one2) + (8 - one3) + 15 * one3 + 7 * one2)
+    pl.semaphore_wait(barrier, 3 + (2 - one2) + (8 - one3) + 15 * one3 + 15 * one2)
 
     def remote(src, dst, send_sem, recv_sem, device):
         return pltpu.make_async_remote_copy(
@@ -192,30 +181,26 @@
     mine2 = pl.ds(pl.multiple_of(32 * place, 32), 32)
     for block in range(4):
         for head in range(HEADS):
-            send(pack3.at[head], in3.at[me], send_in.at[2 * block + head], recv_in.at[4],
-                 16 * block + WORKER3[head])
-    for head in range(HEADS):
-        send(pack2.at[head], work.at[mine2], send_in.at[8 + head], recv_in.at[2],
-             plane + worker2(half, head))
-    send(pack1.at[1 - side], in1.at[mine1], send_in.at[10], recv_in.at[0], partner)
-    other_pair = group + 2 * (1 - pair)
-    for part in range(2):
-        lanes = (slice(0, 256), slice(256, 512))[part]
-        for head in range(HEADS):
-            send(pack2.at[head, :, lanes], work.at[mine2, lanes], send_in.at[11 + 4 * part + head],
-                 recv_in.at[2 + part], plane + worker2(1 - half, head))
-            send(pack1.at[head, :, lanes], in1.at[mine1, lanes], send_in.at[13 + 4 * part + head],
-                 recv_in.at[part], other_pair + head)
-
-    in1[mine1] = pack1[side]
-    for head in range(HEADS):
-        @pl.when(place == WORKER3[head])
-        def _(head=head):
-            in3[me] = pack3[head]
+            send(pack3.at[head], in3.at[me], send_in.at[2 * block + head], recv_in.at[2],
+                 16 * block + worker3[head])
+    for head in range(HEADS):
+        send(pack2.at[head], work.at[mine2], send_in.at[8 + head], recv_in.at[1],
+             plane + worker2[head])
+    for head in range(HEADS):
+        send(pack1.at[head], work.at[mine1], send_in.at[10 + head], recv_in.at[0],
+             group + worker1[head])
+
+    @pl.when(is1)
+    def _():
+        work[mine1] = pack1[head12]
 
     @pl.when(is2)
     def _():
-        work[mine2] = pack2[head2]
+        work[mine2] = pack2[head12]
+
+    @pl.when(is3)
+    def _():
+        in3[me] = pack3[head3]
 
     def unit_refs(unit):
         head = lax.div(unit, 2)
@@ -259,32 +244,68 @@
             target = (row - bases[level]) * RATES[level] + off[level]
             ref[head] = jnp.where(iota((128, TOKENS), 1) == target, 1.0, 0.0).astype(BF16)
 
-    def item_forward(ref, rows, powers_ref, products_ref):
-        scores = nt(ref[:, 0:128], ref[rows, 256:384]) * FACTOR
+    def whole_forward():
+        for chunk in range(2):
+            part = slice(256 * chunk, 256 * chunk + 256)
+            scores = nt(work[:, 0:128], work[part, 256:384]) * FACTOR
+            row_max = jnp.max(scores, 0, keepdims=True)
+            powers = jnp.exp(scores - row_max)
+            weights = powers.astype(BF16)
+            products = nt(work[:, 128:256], work[part, 384:512])
+            power_work[:, part] = powers
+            product_work[:, part] = products
+            stat_work[:, part] = jnp.concatenate(
+                [
+                    row_max,
+                    jnp.sum(powers, 0, keepdims=True),
+                    jnp.sum(weights.astype(F32) * products, 0, keepdims=True),
+                    jnp.zeros((5, 256), F32),
+                ],
+                0,
+            )
+            weighted_work[part] = tn(weights, work[:, 128:256])
+
+    def whole_backward(log_row, delta_row):
+        grad_k = jnp.zeros((KEYS, DIM), F32)
+        grad_v = jnp.zeros((KEYS, DIM), F32)
+        for chunk in range(2):
+            part = slice(256 * chunk, 256 * chunk + 256)
+            log_part, delta_part = log_row[:, part], delta_row[:, part]
+            probs = power_work[:, part] * jnp.exp(stat_work[0:1, part] - log_part)
+            low = (probs * (product_work[:, part] - delta_part)).astype(BF16)
+            grad_work[part, 0:128] = (FACTOR * tn(low, work[:, 0:128])).astype(BF16)
+            grad_k += nn(low, work[part, 256:384])
+            grad_v += nn(probs.astype(BF16), work[part, 384:512])
+        grad_work[:, 128:256] = (FACTOR * grad_k).astype(BF16)
+        grad_work[:, 256:384] = grad_v.astype(BF16)
+
+    rows3 = pl.ds(pl.multiple_of(128 * x, 128), 128)
+
+    def block_forward():
+        scores = nt(work[:, 0:128], work[rows3, 256:384]) * FACTOR
         row_max = jnp.max(scores, 0, keepdims=True)
         powers = jnp.exp(scores - row_max)
-        powers_ref[...] = powers
         weights = powers.astype(BF16)
-        products = nt(ref[:, 128:256], ref[rows, 384:512])
-        products_ref[...] = products
+        products = nt(work[:, 128:256], work[rows3, 384:512])
+        power_work[:, 0:128] = powers
+        product_work[:, 0:128] = products
         stats = jnp.concatenate(
             [
                 row_max,
                 jnp.sum(powers, 0, keepdims=True),
                 jnp.sum(weights.astype(F32) * products, 0, keepdims=True),
-                jnp.zeros((5, row_max.shape[1]), F32),
+                jnp.zeros((5, BLOCK), F32),
             ],
             0,
         )
-        return tn(weights, ref[:, 128:256]), stats
-
-    def item_backward(
-        ref, rows, powers_ref, products_ref, log_all, delta_all, row_max, log_own, delta_own
-    ):
-        k_all, q_all, d_all = ref[:, 0:128], ref[:, 256:384], ref[:, 384:512]
-        k_own, v_own = ref[rows, 0:128], ref[rows, 128:256]
-        probs = powers_ref[...] * jnp.exp(row_max - log_own)
-        low = (probs * (products_ref[...] - delta_own)).astype(BF16)
+        stat_work[:, 0:128] = stats
+        return tn(weights, work[:, 128:256]), stats
+
+    def block_backward(log_all, delta_all, log_own, delta_own):
+        k_all, q_all, d_all = work[:, 0:128], work[:, 256:384], work[:, 384:512]
+        k_own, v_own = work[rows3, 0:128], work[rows3, 128:256]
+        probs = power_work[:, 0:128] * jnp.exp(stat_work[0:1, 0:128] - log_own)
+        low = (probs * (product_work[:, 0:128] - delta_own)).astype(BF16)
         grad_q = FACTOR * tn(low, k_all)
         probs = jnp.exp(nt(k_own, q_all) * FACTOR - log_all)
         low = (probs * (nt(v_own, d_all) - delta_all)).astype(BF16)
@@ -292,33 +313,10 @@
         grad_v = nn(probs.astype(BF16), d_all)
         return jnp.concatenate([grad_q, grad_k, grad_v], 1)
 
-    rows1 = pl.ds(pl.multiple_of(256 * pair, 256), 256)
-    rows2 = pl.ds(pl.multiple_of(256 * half, 256), 256)
-    rows3 = pl.ds(pl.multiple_of(128 * x, 128), 128)
-    power3 = power_work.at[:, 0:128]
-    product3 = product_work.at[:, 0:128]
-
-    @pl.when(is2)
-    def _():
-        arrived(work.at[pl.ds(0, 352)], recv_in.at[2])
-        weighted, stats = item_forward(work, rows2, power_work, product_work)
-        stat_own[:, 0:256] = stats
-        for i in range(8):
-            tile = stats[:, 128 * (i // 4) : 128 * (i // 4) + 128]
-            send2[i] = jnp.concatenate([weighted[32 * i : 32 * i + 32], tile], 0)
-
-    @pl.when(is3)
-    def _():
-        arrived(in3.at[pl.ds(0, 63)], recv_in.at[4])
-        both = in3[...].astype(F32)
-        work[:, 0:256] = both[:, 0:8].reshape(KEYS, 256).astype(BF16)
-        work[:, 256:512] = both[:, 8:16].reshape(KEYS, 256).astype(BF16)
-        weighted, stats = item_forward(work, rows3, power3, product3)
-        stat_own[:, 0:128] = stats
-        for i in range(16):
-            send3[i] = jnp.concatenate([weighted[8 * i : 8 * i + 8], stats], 0)
-
-    def returns(src2, dst2, src3, dst3, sems, recv, wait):
+    def rows_of(ref, index, count):
+        return ref.at[pl.ds(pl.multiple_of(count * index, count), count)]
+
+    def returns(wait, src1, dst1, sem1, recv1, src2, dst2, src3, dst3, sems, recv):
         def each(src, dst, sem, recv_sem, device):
             copy = remote(src, dst, sem, recv_sem, device)
             if wait:
@@ -326,58 +324,114 @@
             else:
                 copy.start()
 
+        if src1 is not None:
+            @pl.when(is1)
+            def _():
+                for i in range(1, 4):
+                    other = lax.rem(y + i, 4)
+                    each(src1(other), dst1(head12), sem1.at[i], recv1.at[head12], group + other)
+
+        if src2 is not None:
+            @pl.when(is2)
+            def _():
+                def step(i, carry):
+                    other = lax.rem(place + i, 16)
+                    each(src2(other), dst2(head12), sems.at[i], recv.at[head12], plane + other)
+                    return carry
+
+                lax.fori_loop(1, 16, step, 0)
+
+            @pl.when(is3)
+            def _():
+                def step(i, carry):
+                    other = lax.rem(place + i, 16)
+                    each(src3(other), dst3(head3), sems.at[i], recv.at[2 + head3], plane + other)
+                    return carry
+
+                lax.fori_loop(1, 16, step, 0)
+
+    def back(wait):
+        returns(
+            wait,
+            lambda i: stat_send.at[i], lambda h: back_stat1.at[h], send_back1, recv_back1,
+            lambda i: send2.at[i], lambda h: back2.at[h],
+            lambda i: send3.at[i], lambda h: back3.at[h], send_back, recv_back,
+        )
+        returns(
+            wait,
+            lambda i: rows_of(weighted_work, i, 128), lambda h: back_rows1.at[h], send_rows1, recv_rows1,
+            None, None, None, None, None, None,
+        )
+
+    def grads_back(wait):
+        returns(
+            wait,
+            lambda i: rows_of(grad_work, i, 128), lambda h: stack.at[h, pl.ds(0, 128)], send_grad1, recv_grad1,
+            lambda i: rows_of(grad_work, i, 32), lambda h: stack.at[h, pl.ds(128, 32)],
+            lambda i: grad_send3.at[i], lambda h: stack.at[h, pl.ds(160, 16)], send_grad, recv_grad,
+        )
+
+    def returned1(dst, recv):
+        for head in range(HEADS):
+            @pl.when(y != worker1[head])
+            def _(head=head):
+                arrived(dst(head), recv.at[head])
+
+    def returned23(dst2, dst3, recv):
+        for head in range(HEADS):
+            @pl.when(place != worker2[head])
+            def _(head=head):
+                arrived(dst2(head), recv.at[head])
+
+            @pl.when(place != worker3[head])
+            def _(head=head):
+                arrived(dst3(head), recv.at[2 + head])
+
+    @pl.when(is1)
+    def _():
+        arrived(work.at[pl.ds(0, 384)], recv_in.at[0])
+
+    @pl.when(is2)
+    def _():
+        arrived(work.at[pl.ds(0, 480)], recv_in.at[1])
+
+    @pl.when(is3)
+    def _():
+        arrived(in3.at[pl.ds(0, 63)], recv_in.at[2])
+        both = in3[...].astype(F32)
+        work[:, 0:256] = both[:, 0:8].reshape(KEYS, 256).astype(BF16)
+        work[:, 256:512] = both[:, 8:16].reshape(KEYS, 256).astype(BF16)
+        weighted, stats = block_forward()
+        for i in range(16):
+            send3[i] = jnp.concatenate([weighted[8 * i : 8 * i + 8], stats], 0)
+        back3[head3] = send3[place]
+
+    @pl.when(is1 | is2)
+    def _():
+        whole_forward()
+        for i in range(4):
+            stat_send[i] = stat_work[:, 128 * i : 128 * i + 128]
+
         @pl.when(is2)
         def _():
-            here = place - 8 * half
-
-            def step(i, carry):
-                other = lax.rem(here + i, 8)
-                each(src2.at[other], dst2.at[head2], sems.at[i], recv.at[head2], plane + 8 * half + other)
-                return carry
-
-            lax.fori_loop(1, 8, step, 0)
-            if not wait:
-                dst2[head2] = src2[here]
-
-        @pl.when(is3)
+            for i in range(16):
+                send2[i, 0:32] = weighted_work[32 * i : 32 * i + 32]
+                send2[i, 32:40] = stat_send[i // 4]
+            back2[head12] = send2[place]
+
+        @pl.when(is1)
         def _():
-            def step(i, carry):
-                other = lax.rem(place + i, 16)
-                each(src3.at[other], dst3.at[head3], sems.at[i], recv.at[2 + head3], plane + other)
-                return carry
-
-            lax.fori_loop(1, 16, step, 0)
-            if not wait:
-                dst3[head3] = src3[place]
-
-    def returned(dst1, dst2, dst3, recv):
-        arrived(dst1.at[1 - side], recv.at[4])
-        for head in range(HEADS):
-            @pl.when(place != worker2(half, head))
-            def _(head=head):
-                arrived(dst2.at[head], recv.at[head])
-
-            @pl.when(place != WORKER3[head])
-            def _(head=head):
-                arrived(dst3.at[head], recv.at[2 + head])
-
-    returns(send2, back2, send3, back3, send_back, recv_back, False)
-
-    arrived(in1.at[:, pl.ds(0, 256)], recv_in.at[0])
-    weighted, stats = item_forward(in1, rows1, power1, product1)
-    stat1[...] = stats
-    for i in range(2):
-        send1[i] = jnp.concatenate(
-            [weighted[128 * i : 128 * i + 128], stats[:, 128 * i : 128 * i + 128]], 0
-        )
-    send(send1.at[1 - side], back1.at[side], send_back.at[16], recv_back.at[4], partner)
-    back1[side] = send1[side]
-
-    returned(back1, back2, back3, recv_back)
+            back_stat1[head12] = stat_send[y]
+            back_rows1[head12] = weighted_work[mine1]
+
+    back(False)
+
+    returned1(lambda h: back_stat1.at[h], recv_back1)
+    returned23(lambda h: back2.at[h], lambda h: back3.at[h], recv_back)
     position = iota((1, TOKENS), 1)
     for head in range(HEADS):
         found = (
-            select_rows(back1[head, 128:136], sel[head, 0:128]),
+            select_rows(back_stat1[head], sel[head, 0:128]),
             select_rows(back2[head, 32:40], sel2[head]),
             select_rows(back3[head, 8:16], sel3[head]),
         )
@@ -408,13 +462,17 @@
     for block in range(4):
         for head in range(HEADS):
             send(tiles.at[2], tiles3.at[me], send_stat.at[2 * block + head], recv_stat.at[2],
-                 16 * block + WORKER3[head])
-    for i in range(4):
-        send(tiles.at[1], tiles2.at[place], send_stat.at[8 + i], recv_stat.at[1],
-             plane + worker2(i // 2, i % 2))
-    for i in range(1, 4):
-        send(tiles.at[0], tiles1.at[y], send_stat.at[11 + i], recv_stat.at[0], group + lax.rem(y + i, 4))
-    tiles1[y] = tiles[0]
+                 16 * block + worker3[head])
+    for head in range(HEADS):
+        send(tiles.at[1], tiles2.at[place], send_stat.at[8 + head], recv_stat.at[1],
+             plane + worker2[head])
+    for head in range(HEADS):
+        send(tiles.at[0], tiles1.at[y], send_stat.at[10 + head], recv_stat.at[0],
+             group + worker1[head])
+
+    @pl.when(is1)
+    def _():
+        tiles1[y] = tiles[0]
 
     @pl.when(is2)
     def _():
@@ -459,54 +517,47 @@
             chosen = jnp.where(block == i, rows[i], chosen)
         return chosen
 
-    def pairs(rows):
-        return [jnp.concatenate(rows[0:2], 1), jnp.concatenate(rows[2:4], 1)]
-
     @pl.when(is2)
     def _():
-        arrived(work.at[pl.ds(0, 128)], recv_in.at[3])
         arrived(tiles2.at[pl.ds(0, 15)], recv_stat.at[1])
-        blocks = [jnp.sum(tiles2[4 * i : 4 * i + 4], 0) for i in range(4)]
-        log_rows, delta_rows = row_blocks(blocks, head2)
-        grads = item_backward(
-            work, rows2, power_work, product_work, jnp.concatenate(log_rows, 1), jnp.concatenate(delta_rows, 1),
-            stat_own[0:1], pick(pairs(log_rows), half), pick(pairs(delta_rows), half),
-        ).astype(BF16)
-        for i in range(8):
-            grad_send2[i] = grads[32 * i : 32 * i + 32]
+        for i in range(4):
+            tiles1[i] = jnp.sum(tiles2[4 * i : 4 * i + 4], 0)
+
+    @pl.when(is1)
+    def _():
+        arrived(tiles1.at[pl.ds(0, 3)], recv_stat.at[0])
+
+    @pl.when(is1 | is2)
+    def _():
+        log_rows, delta_rows = row_blocks([tiles1[i] for i in range(4)], head12)
+        whole_backward(jnp.concatenate(log_rows, 1), jnp.concatenate(delta_rows, 1))
+
+        @pl.when(is2)
+        def _():
+            stack[head12, 128:160] = grad_work[mine2]
+
+        @pl.when(is1)
+        def _():
+            stack[head12, 0:128] = grad_work[mine1]
 
     @pl.when(is3)
     def _():
         arrived(tiles3.at[pl.ds(0, 63)], recv_stat.at[2])
         blocks = [jnp.sum(tiles3[16 * i : 16 * i + 16], 0) for i in range(4)]
         log_rows, delta_rows = row_blocks(blocks, head3)
-        grads = item_backward(
-            work, rows3, power3, product3, jnp.concatenate(log_rows, 1), jnp.concatenate(delta_rows, 1),
-            stat_own[0:1, 0:128], pick(log_rows, x), pick(delta_rows, x),
+        grads = block_backward(
+            jnp.concatenate(log_rows, 1), jnp.concatenate(delta_rows, 1),
+            pick(log_rows, x), pick(delta_rows, x),
         )
         for i in range(16):
             tile = jnp.concatenate([grads[8 * i : 8 * i + 8], jnp.zeros((8, 3 * DIM), F32)], 0)
             grad_send3[i] = tile.astype(BF16)
-
-    stack1 = stack.at[:, 0:128]
-    stack2 = stack.at[:, 128:160]
-    stack3 = stack.at[:, 160:176]
-    returns(grad_send2, stack2, grad_send3, stack3, send_grad, recv_grad, False)
-
-    arrived(in1.at[pl.ds(0, 256), pl.ds(0, 256)], recv_in.at[1])
-    arrived(tiles1.at[pl.ds(0, 3)], recv_stat.at[0])
-    log_rows, delta_rows = row_blocks([tiles1[i] for i in range(4)], side)
-    grads = item_backward(
-        in1, rows1, power1, product1,
-        jnp.concatenate(log_rows, 1), jnp.concatenate(delta_rows, 1),
-        stat1[0:1], pick(pairs(log_rows), pair), pick(pairs(delta_rows), pair),
-    ).astype(BF16)
-    for i in range(2):
-        grad_send1[i] = grads[128 * i : 128 * i + 128]
-    send(grad_send1.at[1 - side], stack1.at[side], send_grad.at[16], recv_grad.at[4], partner)
-    stack1[side] = grad_send1[side]
+        stack[head3, 160:176] = grad_send3[place]
+
+    grads_back(False)
 
     lax.fori_loop(3, 4, backward0, 0)
+    returned1(lambda h: back_rows1.at[h], recv_rows1)
     for head in range(HEADS):
         lane_shares = select_rows_nt(shares[head], sel[head])
         lane = iota((1, 256), 1)
@@ -514,7 +565,7 @@
             lane < 128, lane_shares[1:2], jnp.where(lane < 160, lane_shares[2:3], lane_shares[3:4])
         )
         stacked = jnp.concatenate(
-            [back1[head, 0:128], back2[head, 0:32], back3[head, 0:8], jnp.zeros((88, DIM), F32)], 0
+            [back_rows1[head], back2[head, 0:32], back3[head, 0:8], jnp.zeros((88, DIM), F32)], 0
         ).T * share
         high = stacked.astype(BF16)
         low = (stacked - high.astype(F32)).astype(BF16)
@@ -522,15 +573,18 @@
         att_out[:, DIM * head : DIM * head + DIM] = attended.T
 
     stack_out[:, 176:256] = jnp.zeros((2, 80, 3 * DIM), BF16)
-    returned(stack1, stack2, stack3, recv_grad)
+    returned1(lambda h: stack.at[h, pl.ds(0, 128)], recv_grad1)
+    returned23(
+        lambda h: stack.at[h, pl.ds(128, 32)], lambda h: stack.at[h, pl.ds(160, 16)], recv_grad
+    )
     stack_out[:, 0:176] = stack[...]
 
     for device, copy in pending:
         @pl.when(device != me)
         def _(copy=copy):
             copy.wait_send()
-    returns(send2, back2, send3, back3, send_back, recv_back, True)
-    returns(grad_send2, stack2, grad_send3, stack3, send_grad, recv_grad, True)
+    back(True)
+    grads_back(True)
 
 
 def finish(att, dq, dk, dv, spread, stack, att_out, dq_out, dk_out, dv_out, full, sems):
@@ -588,22 +642,19 @@
             pltpu.VMEM((2, 32, 512), BF16),
             pltpu.VMEM((2, 16, 256), BF16),
             pltpu.VMEM((512, 512), BF16),
-            pltpu.VMEM((512, 512), BF16),
             pltpu.VMEM((64, 16, 256), BF16),
-            pltpu.VMEM((512, 256), F32),
-            pltpu.VMEM((512, 256), F32),
-            pltpu.VMEM((512, 256), F32),
-            pltpu.VMEM((512, 256), F32),
-            pltpu.VMEM((8, 256), F32),
-            pltpu.VMEM((8, 256), F32),
-            pltpu.VMEM((2, 136, 128), F32),
-            pltpu.VMEM((8, 40, 128), F32),
+            pltpu.VMEM((512, 512), F32),
+            pltpu.VMEM((512, 512), F32),
+            pltpu.VMEM((8, 512), F32),
+            pltpu.VMEM((512, 128), F32),
+            pltpu.VMEM((4, 8, 128), F32),
+            pltpu.VMEM((16, 40, 128), F32),
             pltpu.VMEM((16, 16, 128), F32),
-            pltpu.VMEM((2, 136, 128), F32),
+            pltpu.VMEM((2, 8, 128), F32),
+            pltpu.VMEM((2, 128, 128), F32),
             pltpu.VMEM((2, 40, 128), F32),
             pltpu.VMEM((2, 16, 128), F32),
-            pltpu.VMEM((2, 128, 384), BF16),
-            pltpu.VMEM((8, 32, 384), BF16),
+            pltpu.VMEM((512, 384), BF16),
             pltpu.VMEM((16, 16, 384), BF16),
             pltpu.VMEM((2, 176, 384), BF16),
             pltpu.VMEM((3, 8, 128), F32),
@@ -611,14 +662,20 @@
             pltpu.VMEM((16, 8, 128), F32),
             pltpu.VMEM((64, 8, 128), F32),
             dma((5,)),
-            dma((19,)),
-            dma((17,)),
-            dma((15,)),
-            dma((17,)),
-            dma((5,)),
-            dma((5,)),
+            dma((12,)),
+            dma((16,)),
+            dma((4,)),
+            dma((4,)),
+            dma((12,)),
+            dma((16,)),
+            dma((4,)),
             dma((3,)),
-            dma((5,)),
+            dma((4,)),
+            dma((2,)),
+            dma((2,)),
+            dma((3,)),
+            dma((4,)),
+            dma((2,)),
         ],
         compiler_params=pltpu.CompilerParams(
             collective_id=0, has_side_effects=True, vmem_limit_bytes=32 * 2**20

time: 38.5 us -> 36.7 us (0.953)
  the two profiles are of different devices: /device:TPU:8 before, /device:TPU:24 now
where the time goes in v4:
time: 36.7 us; the launch traced here: 36.6 us
  Pallas kernels  36 us (98%)
  between operations  0.64 us (2%)
    pallas_call x1, Pallas kernels, body(): pl.pallas_call(kernel, out_shape=(out, out, out, out, jax.ShapeDtypeStruc...  33.8 us
    pallas_call x1, Pallas kernels, body(): pl.pallas_call(finish, out_shape=(out, out, out, out), in_specs=[vmem] *...  2.13 us

profile of v4, /device:TPU:24, one launch (start us, length us, event | category | flops | bytes accessed | tf_op | source)
XLA Modules:
  0.0 36.6 jit_solution(14577420382101018388)
XLA Ops:
  0.6 33.8 %shard_map.84 = (f32[1024,256]{1,0:T(8,128)S(1)}, f32[1024,256]{1,0:T(8,128)S(1)}, f32[1024,256]{1,0:T(8,128)S(1)}, f32[1024,256]{1,0:T(8,128)S(1)}, bf16[2,1024...) custom-call(s32[2,3]{1,0:T(2,128)} %bitcast.1, bf16[1024,256]{1,0:T(8,128)(2,1)} %query_hbm.1, ...), custom_call_target="tpu_custom_call" | custom-call | tf_op jit(solution)/shard_map/pallas_call | solution.py:620
  34.5 2.1 %shard_map.85 = (f32[1024,256]{1,0:T(8,128)}, f32[1024,256]{1,0:T(8,128)}, f32[1024,256]{1,0:T(8,128)}, f32[1024,256]{1,0:T(8,128)}) custom-call(f32[1024,256]{1,0:T(8,128)S(1)} %get-tuple-element.10.att, f32[1024,256]{1,0:T(8,128)S(1)} %get-tuple-element.11.dq, f32[1024,256]{1,0:T(8,128)S(1)} %get-tuple-element.12.dk, ...), custom_call_target="tpu_custom_call" | custom-call | tf_op jit(solution)/shard_map/pallas_call | solution.py:684

commit v5 on v4

--- a/solution.py
+++ b/solution.py
@@ -65,9 +65,9 @@
     sel, sel2, sel3, powers0, products0, shares, weighted0, stat0, logs,
     pack1, pack2, pack3, work, in3, power_work, product_work, stat_work, weighted_work,
     stat_send, send2, send3, back_stat1, back_rows1, back2, back3, grad_work, grad_send3, stack,
-    tiles, tiles1, tiles2, tiles3,
+    tiles, tiles1, tiles2, tiles3, shared, swap_send, swap1, swap2, swap3,
     load_sem, send_in, send_back, send_back1, send_rows1, send_stat, send_grad, send_grad1,
-    recv_in, recv_back, recv_back1, recv_rows1, recv_stat, recv_grad, recv_grad1,
+    recv_in, recv_back, recv_back1, recv_rows1, recv_stat, recv_grad, recv_grad1, send_swap, recv_swap,
 ):
     me = lax.axis_index("seq")
     y = lax.rem(me, 4)
@@ -227,6 +227,7 @@
             stat0[head, 2:3, part] = jnp.sum(weights.astype(F32) * products, 0, keepdims=True)
         return carry
 
+    stat0[...] = jnp.zeros_like(stat0)
     lax.fori_loop(0, 4, forward0, 0)
     for head in range(HEADS):
         off = [offsets[head, level] for level in range(3)]
@@ -243,6 +244,67 @@
         for ref, level in ((sel2, 1), (sel3, 2)):
             target = (row - bases[level]) * RATES[level] + off[level]
             ref[head] = jnp.where(iota((128, TOKENS), 1) == target, 1.0, 0.0).astype(BF16)
+
+    for head in range(HEADS):
+        for level, chooser in enumerate((sel[head, 0:128], sel2[head], sel3[head])):
+            tiles[level, 3 * head : 3 * head + 3] = select_rows_nt(stat0[head], chooser)[0:3]
+    for level in range(3):
+        tiles[level, 6:8] = jnp.zeros((2, BLOCK), F32)
+    for block in range(4):
+        for head in range(HEADS):
+            send(tiles.at[2], tiles3.at[me], send_stat.at[2 * block + head], recv_stat.at[2],
+                 16 * block + worker3[head])
+    for head in range(HEADS):
+        send(tiles.at[1], tiles2.at[place], send_stat.at[8 + head], recv_stat.at[1],
+             plane + worker2[head])
+    for head in range(HEADS):
+        send(tiles.at[0], tiles1.at[y], send_stat.at[10 + head], recv_stat.at[0],
+             group + worker1[head])
+
+    @pl.when(is1)
+    def _():
+        tiles1[y] = tiles[0]
+
+    @pl.when(is2)
+    def _():
+        tiles2[place] = tiles[1]
+
+    @pl.when(is3)
+    def _():
+        tiles3[me] = tiles[2]
+
+    worker_head = jnp.where(is3, head3, head12)
+    off1, off2, off3 = (
+        jnp.where(worker_head == 0, offsets[0, level], offsets[1, level]) for level in range(3)
+    )
+    column = iota((1, KEYS), 1)
+    row = iota((BLOCK, 1), 0)
+    own_position = jnp.where(
+        is1, column * RATES[0] + off1, jnp.where(is2, column * RATES[1] + off2, column * RATES[2] + off3)
+    )
+    shared[0] = jnp.where(
+        column * RATES[0] + off1 == row * RATES[1] + off2, 1.0, 0.0
+    ).astype(BF16)
+    in_plane = own_position + jnp.where(is1, 4 * TOKENS * z, 0)
+    shared[1] = jnp.where(in_plane == row * RATES[2] + off3, 1.0, 0.0).astype(BF16)
+    members = [
+        lax.rem(own_position, rate) == off for rate, off in zip(RATES, (off1, off2, off3))
+    ]
+
+    def merge(items):
+        peak = items[0][0]
+        for item in items[1:]:
+            peak = jnp.maximum(peak, item[0])
+        factors = [jnp.exp(item[0] - peak) for item in items]
+        total = factors[0] * items[0][1]
+        product = factors[0] * items[0][2]
+        for factor, item in zip(factors[1:], items[1:]):
+            total += factor * item[1]
+            product += factor * item[2]
+        return peak, total, product
+
+    def of_level(rows, member):
+        return jnp.where(member, rows[0:1], -jnp.inf), rows[1:2], rows[2:3]
 
     def whole_forward():
         for chunk in range(2):
@@ -424,7 +486,133 @@
             back_stat1[head12] = stat_send[y]
             back_rows1[head12] = weighted_work[mine1]
 
+    def exchange(wait):
+        def each(src, dst, slot, device):
+            copy = remote(src, dst, send_swap.at[slot], recv_swap.at[0], device)
+            if wait:
+                copy.wait_send()
+            else:
+                copy.start()
+
+        @pl.when(is1)
+        def _():
+            for block in range(4):
+                device = 16 * block + jnp.where(head12 == 0, worker3[0], worker3[1])
+                each(swap_send.at[1], swap3.at[4 * x + z], block, device)
+            device = plane + jnp.where(head12 == 0, worker2[0], worker2[1])
+            each(swap_send.at[0], swap2.at[z], 4, device)
+
+        @pl.when(is2)
+        def _():
+            for block in range(4):
+                device = 16 * block + jnp.where(head12 == 0, worker3[0], worker3[1])
+                each(swap_send.at[1], swap3.at[16 + x], block, device)
+            for block in range(4):
+                device = plane + 4 * block + jnp.where(head12 == 0, worker1[0], worker1[1])
+                each(stat_send.at[block], swap1.at[0], 4 + block, device)
+
+        @pl.when(is3)
+        def _():
+            for i in range(1, 4):
+                device = 16 * lax.rem(x + i, 4) + place
+                each(swap_send.at[0], swap3.at[20 + x], i, device)
+            for block in range(4):
+                device = plane + 4 * block + jnp.where(head3 == 0, worker1[0], worker1[1])
+                each(swap_send.at[0], swap1.at[1], 4 + block, device)
+            device = plane + jnp.where(head3 == 0, worker2[0], worker2[1])
+            each(swap_send.at[0], swap2.at[4], 0, device)
+
+    @pl.when(is1)
+    def _():
+        swap_send[0] = select_rows_nt(stat_work[...], shared[0])
+
+    @pl.when(is1 | is2)
+    def _():
+        swap_send[1] = select_rows_nt(stat_work[...], shared[1])
+
+    @pl.when(is3)
+    def _():
+        swap_send[0] = stat_work[:, 0:128]
+        swap3[20 + x] = stat_work[:, 0:128]
+
+    exchange(False)
     back(False)
+
+    def below_rows(blocks, head):
+        rows = jnp.concatenate(blocks, 1)
+        return [jnp.where(head == 0, rows[i : i + 1], rows[3 + i : 4 + i]) for i in range(3)]
+
+    def final_rows(items):
+        peak, total, product = merge(items)
+        return peak + jnp.log(total), product / total
+
+    def blocks_of(row):
+        return [row[:, i : i + BLOCK] for i in range(0, KEYS, BLOCK)]
+
+    def pick(rows, block):
+        chosen = rows[0]
+        for i in range(1, len(rows)):
+            chosen = jnp.where(block == i, rows[i], chosen)
+        return chosen
+
+    @pl.when(is2)
+    def _():
+        arrived(tiles2.at[pl.ds(0, 15)], recv_stat.at[1])
+        arrived(swap2, recv_swap.at[0])
+        for i in range(4):
+            tiles1[i] = jnp.sum(tiles2[4 * i : 4 * i + 4], 0)
+
+    @pl.when(is1)
+    def _():
+        arrived(tiles1.at[pl.ds(0, 3)], recv_stat.at[0])
+        arrived(swap1, recv_swap.at[0])
+
+    @pl.when(is1 | is2)
+    def _():
+        below = below_rows([tiles1[i] for i in range(4)], head12)
+        own = [stat_work[i : i + 1] for i in range(3)]
+        lacking = jnp.where(
+            is1, select_rows(swap1[0], shared[0]), jnp.concatenate([swap2[i] for i in range(4)], 1)
+        )
+        member = (is1 & members[1]) | (is2 & members[0])
+        level3 = select_rows(jnp.where(is1, swap1[1], swap2[4]), shared[1])
+        whole_backward(
+            *final_rows([below, own, of_level(lacking, member), of_level(level3, members[2])])
+        )
+
+        @pl.when(is2)
+        def _():
+            stack[head12, 128:160] = grad_work[mine2]
+
+        @pl.when(is1)
+        def _():
+            stack[head12, 0:128] = grad_work[mine1]
+
+    @pl.when(is3)
+    def _():
+        arrived(tiles3.at[pl.ds(0, 63)], recv_stat.at[2])
+        arrived(swap3.at[pl.ds(0, 23)], recv_swap.at[0])
+        below = below_rows([jnp.sum(tiles3[16 * i : 16 * i + 16], 0) for i in range(4)], head3)
+        own = jnp.concatenate([swap3[20 + i] for i in range(4)], 1)
+        level1 = jnp.concatenate([jnp.sum(swap3[4 * i : 4 * i + 4], 0) for i in range(4)], 1)
+        level2 = jnp.concatenate([swap3[16 + i] for i in range(4)], 1)
+        log_row, delta_row = final_rows(
+            [
+                below,
+                [own[i : i + 1] for i in range(3)],
+                of_level(level1, members[0]),
+                of_level(level2, members[1]),
+            ]
+        )
+        grads = block_backward(
+            log_row, delta_row, pick(blocks_of(log_row), x), pick(blocks_of(delta_row), x)
+        )
+        for i in range(16):
+            tile = jnp.concatenate([grads[8 * i : 8 * i + 8], jnp.zeros((8, 3 * DIM), F32)], 0)
+            grad_send3[i] = tile.astype(BF16)
+        stack[head3, 160:176] = grad_send3[place]
+
+    grads_back(False)
 
     returned1(lambda h: back_stat1.at[h], recv_back1)
     returned23(lambda h: back2.at[h], lambda h: back3.at[h], recv_back)
@@ -435,52 +623,18 @@
             select_rows(back2[head, 32:40], sel2[head]),
             select_rows(back3[head, 8:16], sel3[head]),
         )
-        maxima = [stat0[head, 0:1]]
+        items = [[stat0[head, i : i + 1] for i in range(3)]]
         for level in range(3):
             member = lax.rem(position, RATES[level]) == offsets[head, level]
-            maxima.append(jnp.where(member, found[level][0:1], -jnp.inf))
-        peak = jnp.maximum(jnp.maximum(maxima[0], maxima[1]), jnp.maximum(maxima[2], maxima[3]))
-        factors = [jnp.exp(item - peak) for item in maxima]
-        denominator = factors[0] * stat0[head, 1:2]
-        for level in range(3):
-            denominator += factors[level + 1] * found[level][1:2]
-        product = factors[0] * stat0[head, 2:3]
-        for level in range(3):
-            product += factors[level + 1] * found[level][2:3]
-        log_total = peak + jnp.log(denominator)
-        inverse = 1.0 / denominator
-        rows = jnp.concatenate([log_total, product * inverse, jnp.zeros((6, TOKENS), F32)], 0)
-        logs[head] = rows
+            items.append(of_level(found[level], member))
+        peak, total, product = merge(items)
+        inverse = 1.0 / total
+        logs[head] = jnp.concatenate(
+            [peak + jnp.log(total), product * inverse, jnp.zeros((6, TOKENS), F32)], 0
+        )
         shares[head] = jnp.concatenate(
-            [item * inverse for item in factors] + [jnp.zeros((4, TOKENS), F32)], 0
-        )
-        for level, chooser in enumerate((sel[head, 0:128], sel2[head], sel3[head])):
-            tiles[level, 2 * head : 2 * head + 2] = select_rows_nt(rows, chooser)[0:2]
-    for level in range(3):
-        tiles[level, 4:8] = jnp.zeros((4, BLOCK), F32)
-
-    for block in range(4):
-        for head in range(HEADS):
-            send(tiles.at[2], tiles3.at[me], send_stat.at[2 * block + head], recv_stat.at[2],
-                 16 * block + worker3[head])
-    for head in range(HEADS):
-        send(tiles.at[1], tiles2.at[place], send_stat.at[8 + head], recv_stat.at[1],
-             plane + worker2[head])
-    for head in range(HEADS):
-        send(tiles.at[0], tiles1.at[y], send_stat.at[10 + head], recv_stat.at[0],
-             group + worker1[head])
-
-    @pl.when(is1)
-    def _():
-        tiles1[y] = tiles[0]
-
-    @pl.when(is2)
-    def _():
-        tiles2[place] = tiles[1]
-
-    @pl.when(is3)
-    def _():
-        tiles3[me] = tiles[2]
+            [jnp.exp(item[0] - peak) * inverse for item in items] + [jnp.zeros((4, TOKENS), F32)], 0
+        )
 
     def backward0(unit, carry):
         head, segment, lanes = unit_refs(unit)
@@ -502,61 +656,8 @@
         dv_out[rows, lanes] = grad_v
         return carry
 
-    lax.fori_loop(0, 3, backward0, 0)
-
-    def row_blocks(blocks, head):
-        first = head == 0
-        return (
-            [jnp.where(first, tile[0:1], tile[2:3]) for tile in blocks],
-            [jnp.where(first, tile[1:2], tile[3:4]) for tile in blocks],
-        )
-
-    def pick(rows, block):
-        chosen = rows[0]
-        for i in range(1, len(rows)):
-            chosen = jnp.where(block == i, rows[i], chosen)
-        return chosen
-
-    @pl.when(is2)
-    def _():
-        arrived(tiles2.at[pl.ds(0, 15)], recv_stat.at[1])
-        for i in range(4):
-            tiles1[i] = jnp.sum(tiles2[4 * i : 4 * i + 4], 0)
-
-    @pl.when(is1)
-    def _():
-        arrived(tiles1.at[pl.ds(0, 3)], recv_stat.at[0])
-
-    @pl.when(is1 | is2)
-    def _():
-        log_rows, delta_rows = row_blocks([tiles1[i] for i in range(4)], head12)
-        whole_backward(jnp.concatenate(log_rows, 1), jnp.concatenate(delta_rows, 1))
-
-        @pl.when(is2)
-        def _():
-            stack[head12, 128:160] = grad_work[mine2]
-
-        @pl.when(is1)
-        def _():
-            stack[head12, 0:128] = grad_work[mine1]
-
-    @pl.when(is3)
-    def _():
-        arrived(tiles3.at[pl.ds(0, 63)], recv_stat.at[2])
-        blocks = [jnp.sum(tiles3[16 * i : 16 * i + 16], 0) for i in range(4)]
-        log_rows, delta_rows = row_blocks(blocks, head3)
-        grads = block_backward(
-            jnp.concatenate(log_rows, 1), jnp.concatenate(delta_rows, 1),
-            pick(log_rows, x), pick(delta_rows, x),
-        )
-        for i in range(16):
-            tile = jnp.concatenate([grads[8 * i : 8 * i + 8], jnp.zeros((8, 3 * DIM), F32)], 0)
-            grad_send3[i] = tile.astype(BF16)
-        stack[head3, 160:176] = grad_send3[place]
-
-    grads_back(False)
-
-    lax.fori_loop(3, 4, backward0, 0)
+    lax.fori_loop(0, 4, backward0, 0)
+
     returned1(lambda h: back_rows1.at[h], recv_rows1)
     for head in range(HEADS):
         lane_shares = select_rows_nt(shares[head], sel[head])
@@ -583,6 +684,7 @@
         @pl.when(device != me)
         def _(copy=copy):
             copy.wait_send()
+    exchange(True)
     back(True)
     grads_back(True)
 
@@ -661,6 +763,11 @@
             pltpu.VMEM((4, 8, 128), F32),
             pltpu.VMEM((16, 8, 128), F32),
             pltpu.VMEM((64, 8, 128), F32),
+            pltpu.VMEM((2, 128, KEYS), BF16),
+            pltpu.VMEM((2, 8, 128), F32),
+            pltpu.VMEM((2, 8, 128), F32),
+            pltpu.VMEM((5, 8, 128), F32),
+            pltpu.VMEM((24, 8, 128), F32),
             dma((5,)),
             dma((12,)),
             dma((16,)),
@@ -676,6 +783,8 @@
             dma((3,)),
             dma((4,)),
             dma((2,)),
+            dma((8,)),
+            dma((1,)),
         ],
         compiler_params=pltpu.CompilerParams(
             collective_id=0, has_side_effects=True, vmem_limit_bytes=32 * 2**20

time: 36.7 us -> 31.8 us (0.87)
  the two profiles are of different devices: /device:TPU:24 before, /device:TPU:8 now
where the time goes in v5:
time: 31.8 us; the launch traced here: 31.7 us
  Pallas kernels  31 us (97%)
  between operations  0.64 us (2%)
    pallas_call x1, Pallas kernels, body(): pl.pallas_call(kernel, out_shape=(out, out, out, out, jax.ShapeDtypeStruc...  28.9 us
    pallas_call x1, Pallas kernels, body(): pl.pallas_call(finish, out_shape=(out, out, out, out), in_specs=[vmem] *...  2.13 us

profile of v5, /device:TPU:8, one launch (start us, length us, event | category | flops | bytes accessed | tf_op | source)
XLA Modules:
  0.0 31.7 jit_solution(4872470499672203004)
XLA Ops:
  0.6 28.9 %shard_map.84 = (f32[1024,256]{1,0:T(8,128)S(1)}, f32[1024,256]{1,0:T(8,128)S(1)}, f32[1024,256]{1,0:T(8,128)S(1)}, f32[1024,256]{1,0:T(8,128)S(1)}, bf16[2,1024...) custom-call(s32[2,3]{1,0:T(2,128)} %bitcast.1, bf16[1024,256]{1,0:T(8,128)(2,1)} %query_hbm.1, ...), custom_call_target="tpu_custom_call" | custom-call | tf_op jit(solution)/shard_map/pallas_call | solution.py:722
  29.5 2.1 %shard_map.85 = (f32[1024,256]{1,0:T(8,128)}, f32[1024,256]{1,0:T(8,128)}, f32[1024,256]{1,0:T(8,128)}, f32[1024,256]{1,0:T(8,128)}) custom-call(f32[1024,256]{1,0:T(8,128)S(1)} %get-tuple-element.10.att, f32[1024,256]{1,0:T(8,128)S(1)} %get-tuple-element.11.dq, f32[1024,256]{1,0:T(8,128)S(1)} %get-tuple-element.12.dk, ...), custom_call_target="tpu_custom_call" | custom-call | tf_op jit(solution)/shard_map/pallas_call | solution.py:793

commit v6 on v5

--- a/solution.py
+++ b/solution.py
@@ -62,7 +62,7 @@
     offsets_hbm, query_hbm, keys_hbm, values_hbm, dout_hbm,
     att_out, dq_out, dk_out, dv_out, spread, stack_out,
     offsets, query, keys, values, dout,
-    sel, sel2, sel3, powers0, products0, shares, weighted0, stat0, logs,
+    small, wide3, sel, sel2, sel3, powers0, products0, shares, weighted0, stat0, logs,
     pack1, pack2, pack3, work, in3, power_work, product_work, stat_work, weighted_work,
     stat_send, send2, send3, back_stat1, back_rows1, back2, back3, grad_work, grad_send3, stack,
     tiles, tiles1, tiles2, tiles3, shared, swap_send, swap1, swap2, swap3,
@@ -92,7 +92,7 @@
     load_offsets.start()
     loads = []
     for i, (source, held) in enumerate(
-        ((query_hbm, query), (keys_hbm, keys), (values_hbm, values), (dout_hbm, dout))
+        ((keys_hbm, keys), (values_hbm, values), (query_hbm, query), (dout_hbm, dout))
     ):
         loads.append(pltpu.make_async_copy(source, held, load_sem.at[i]))
         loads[-1].start()
@@ -126,35 +126,37 @@
     for i in range(1, 4):
         greet(group + lax.rem(y + i, 4))
 
-    bases = (0, 32 * y, 8 * place)
     load_offsets.wait()
+    row = iota((48, 1), 0)
     for head in range(HEADS):
         off = [offsets[head, level] for level in range(3)]
-
-        def target(index, off=off):
-            return jnp.where(
-                index < 128,
-                index * RATES[0] + off[0],
+        for part in range(4):
+            target = jnp.where(
+                row < 32,
+                row * RATES[0] + off[0],
                 jnp.where(
-                    index < 160, (index - 128) * RATES[1] + off[1], (index - 160) * RATES[2] + off[2]
+                    row < 40, (row - 32) * RATES[1] + off[1], (row - 40 - 2 * part) * RATES[2] + off[2]
                 ),
             )
-
-        sel[head] = jnp.where(
-            iota((256, TOKENS), 1) == target(iota((256, 1), 0)), 1.0, 0.0
-        ).astype(BF16)
-    for load in loads:
-        load.wait()
-    for head in range(HEADS):
-        lanes = slice(DIM * head, DIM * head + DIM)
-        chooser = sel[head, 0:176]
-        first = nn(chooser, jnp.concatenate([keys[:, lanes], values[:, lanes]], 1))
-        second = nn(chooser, jnp.concatenate([query[:, lanes], dout[:, lanes]], 1))
-        pack1[head, :, 0:256] = first[:128].astype(BF16)
-        pack1[head, :, 256:512] = second[:128].astype(BF16)
-        pack2[head, :, 0:256] = first[128:160].astype(BF16)
-        pack2[head, :, 256:512] = second[128:160].astype(BF16)
-        pack3[head] = jnp.concatenate([first[160:168], second[160:168]], 0).astype(BF16)
+            small[head, part] = jnp.where(iota((48, 256), 1) == target, 1.0, 0.0).astype(BF16)
+    for pair, sources in enumerate(((keys, values), (query, dout))):
+        for load in loads[2 * pair : 2 * pair + 2]:
+            load.wait()
+        wide = slice(256 * pair, 256 * pair + 256)
+        for head in range(HEADS):
+            lanes = slice(DIM * head, DIM * head + DIM)
+            pieces = []
+            for part in range(4):
+                rows = slice(256 * part, 256 * part + 256)
+                both = jnp.concatenate([source[rows, lanes] for source in sources], 1)
+                pieces.append(nn(small[head, part], both))
+                pack1[head, 32 * part : 32 * part + 32, wide] = pieces[part][0:32].astype(BF16)
+            pack2[head, :, wide] = jnp.concatenate([piece[32:40] for piece in pieces], 0).astype(BF16)
+            wide3[head, 8 * pair : 8 * pair + 8] = (
+                (pieces[0][40:48] + pieces[1][40:48]) + (pieces[2][40:48] + pieces[3][40:48])
+            )
+    for head in range(HEADS):
+        pack3[head] = wide3[head].astype(BF16)
 
     pl.semaphore_wait(barrier, 3 + (2 - one2) + (8 - one3) + 15 * one3 + 15 * one2)
 
@@ -164,11 +166,8 @@
             device_id={"seq": device}, device_id_type=MESH,
         )
 
-    pending = []
-
     def send(src, dst, send_sem, recv_sem, device):
         copy = remote(src, dst, send_sem, recv_sem, device)
-        pending.append((device, copy))
 
         @pl.when(device != me)
         def _():
@@ -179,16 +178,16 @@
 
     mine1 = pl.ds(pl.multiple_of(128 * y, 128), 128)
     mine2 = pl.ds(pl.multiple_of(32 * place, 32), 32)
+    for head in range(HEADS):
+        send(pack1.at[head], work.at[mine1], send_in.at[0], recv_in.at[0],
+             group + worker1[head])
     for block in range(4):
         for head in range(HEADS):
-            send(pack3.at[head], in3.at[me], send_in.at[2 * block + head], recv_in.at[2],
+            send(pack3.at[head], in3.at[me], send_in.at[2], recv_in.at[2],
                  16 * block + worker3[head])
     for head in range(HEADS):
-        send(pack2.at[head], work.at[mine2], send_in.at[8 + head], recv_in.at[1],
+        send(pack2.at[head], work.at[mine2], send_in.at[1], recv_in.at[1],
              plane + worker2[head])
-    for head in range(HEADS):
-        send(pack1.at[head], work.at[mine1], send_in.at[10 + head], recv_in.at[0],
-             group + worker1[head])
 
     @pl.when(is1)
     def _():
@@ -229,21 +228,26 @@
 
     stat0[...] = jnp.zeros_like(stat0)
     lax.fori_loop(0, 4, forward0, 0)
+    bases = (0, 32 * y, 8 * place)
+
+    def target(index, off):
+        return jnp.where(
+            index < 128,
+            index * RATES[0] + off[0],
+            jnp.where(
+                index < 160, (index - 128) * RATES[1] + off[1], (index - 160) * RATES[2] + off[2]
+            ),
+        )
+
     for head in range(HEADS):
         off = [offsets[head, level] for level in range(3)]
-        column = iota((1, 256), 1)
-        target = jnp.where(
-            column < 128,
-            column * RATES[0] + off[0],
-            jnp.where(
-                column < 160, (column - 128) * RATES[1] + off[1], (column - 160) * RATES[2] + off[2]
-            ),
-        )
-        spread[head] = jnp.where(iota((TOKENS, 256), 0) == target, 1.0, 0.0).astype(BF16)
+        sel[head] = jnp.where(
+            iota((256, TOKENS), 1) == target(iota((256, 1), 0), off), 1.0, 0.0
+        ).astype(BF16)
         row = iota((128, 1), 0)
         for ref, level in ((sel2, 1), (sel3, 2)):
-            target = (row - bases[level]) * RATES[level] + off[level]
-            ref[head] = jnp.where(iota((128, TOKENS), 1) == target, 1.0, 0.0).astype(BF16)
+            wanted = (row - bases[level]) * RATES[level] + off[level]
+            ref[head] = jnp.where(iota((128, TOKENS), 1) == wanted, 1.0, 0.0).astype(BF16)
 
     for head in range(HEADS):
         for level, chooser in enumerate((sel[head, 0:128], sel2[head], sel3[head])):
@@ -252,13 +256,13 @@
         tiles[level, 6:8] = jnp.zeros((2, BLOCK), F32)
     for block in range(4):
         for head in range(HEADS):
-            send(tiles.at[2], tiles3.at[me], send_stat.at[2 * block + head], recv_stat.at[2],
+            send(tiles.at[2], tiles3.at[me], send_stat.at[2], recv_stat.at[2],
                  16 * block + worker3[head])
     for head in range(HEADS):
-        send(tiles.at[1], tiles2.at[place], send_stat.at[8 + head], recv_stat.at[1],
+        send(tiles.at[1], tiles2.at[place], send_stat.at[1], recv_stat.at[1],
              plane + worker2[head])
     for head in range(HEADS):
-        send(tiles.at[0], tiles1.at[y], send_stat.at[10 + head], recv_stat.at[0],
+        send(tiles.at[0], tiles1.at[y], send_stat.at[0], recv_stat.at[0],
              group + worker1[head])
 
     @pl.when(is1)
@@ -378,27 +382,23 @@
     def rows_of(ref, index, count):
         return ref.at[pl.ds(pl.multiple_of(count * index, count), count)]
 
-    def returns(wait, src1, dst1, sem1, recv1, src2, dst2, src3, dst3, sems, recv):
+    def returns(src1, dst1, sem1, recv1, src2, dst2, src3, dst3, sems, recv):
         def each(src, dst, sem, recv_sem, device):
-            copy = remote(src, dst, sem, recv_sem, device)
-            if wait:
-                copy.wait_send()
-            else:
-                copy.start()
+            remote(src, dst, sem.at[0], recv_sem, device).start()
 
         if src1 is not None:
             @pl.when(is1)
             def _():
                 for i in range(1, 4):
                     other = lax.rem(y + i, 4)
-                    each(src1(other), dst1(head12), sem1.at[i], recv1.at[head12], group + other)
+                    each(src1(other), dst1(head12), sem1, recv1.at[head12], group + other)
 
         if src2 is not None:
             @pl.when(is2)
             def _():
                 def step(i, carry):
                     other = lax.rem(place + i, 16)
-                    each(src2(other), dst2(head12), sems.at[i], recv.at[head12], plane + other)
+                    each(src2(other), dst2(head12), sems, recv.at[head12], plane + other)
                     return carry
 
                 lax.fori_loop(1, 16, step, 0)
@@ -407,27 +407,24 @@
             def _():
                 def step(i, carry):
                     other = lax.rem(place + i, 16)
-                    each(src3(other), dst3(head3), sems.at[i], recv.at[2 + head3], plane + other)
+                    each(src3(other), dst3(head3), sems, recv.at[2 + head3], plane + other)
                     return carry
 
                 lax.fori_loop(1, 16, step, 0)
 
-    def back(wait):
+    def back():
         returns(
-            wait,
             lambda i: stat_send.at[i], lambda h: back_stat1.at[h], send_back1, recv_back1,
             lambda i: send2.at[i], lambda h: back2.at[h],
             lambda i: send3.at[i], lambda h: back3.at[h], send_back, recv_back,
         )
         returns(
-            wait,
             lambda i: rows_of(weighted_work, i, 128), lambda h: back_rows1.at[h], send_rows1, recv_rows1,
             None, None, None, None, None, None,
         )
 
-    def grads_back(wait):
+    def grads_back():
         returns(
-            wait,
             lambda i: rows_of(grad_work, i, 128), lambda h: stack.at[h, pl.ds(0, 128)], send_grad1, recv_grad1,
             lambda i: rows_of(grad_work, i, 32), lambda h: stack.at[h, pl.ds(128, 32)],
             lambda i: grad_send3.at[i], lambda h: stack.at[h, pl.ds(160, 16)], send_grad, recv_grad,
@@ -486,41 +483,37 @@
             back_stat1[head12] = stat_send[y]
             back_rows1[head12] = weighted_work[mine1]
 
-    def exchange(wait):
-        def each(src, dst, slot, device):
-            copy = remote(src, dst, send_swap.at[slot], recv_swap.at[0], device)
-            if wait:
-                copy.wait_send()
-            else:
-                copy.start()
+    def exchange():
+        def each(src, dst, device):
+            remote(src, dst, send_swap.at[0], recv_swap.at[0], device).start()
 
         @pl.when(is1)
         def _():
             for block in range(4):
                 device = 16 * block + jnp.where(head12 == 0, worker3[0], worker3[1])
-                each(swap_send.at[1], swap3.at[4 * x + z], block, device)
+                each(swap_send.at[1], swap3.at[4 * x + z], device)
             device = plane + jnp.where(head12 == 0, worker2[0], worker2[1])
-            each(swap_send.at[0], swap2.at[z], 4, device)
+            each(swap_send.at[0], swap2.at[z], device)
 
         @pl.when(is2)
         def _():
             for block in range(4):
                 device = 16 * block + jnp.where(head12 == 0, worker3[0], worker3[1])
-                each(swap_send.at[1], swap3.at[16 + x], block, device)
+                each(swap_send.at[1], swap3.at[16 + x], device)
             for block in range(4):
                 device = plane + 4 * block + jnp.where(head12 == 0, worker1[0], worker1[1])
-                each(stat_send.at[block], swap1.at[0], 4 + block, device)
+                each(stat_send.at[block], swap1.at[0], device)
 
         @pl.when(is3)
         def _():
             for i in range(1, 4):
                 device = 16 * lax.rem(x + i, 4) + place
-                each(swap_send.at[0], swap3.at[20 + x], i, device)
+                each(swap_send.at[0], swap3.at[20 + x], device)
             for block in range(4):
                 device = plane + 4 * block + jnp.where(head3 == 0, worker1[0], worker1[1])
-                each(swap_send.at[0], swap1.at[1], 4 + block, device)
+                each(swap_send.at[0], swap1.at[1], device)
             device = plane + jnp.where(head3 == 0, worker2[0], worker2[1])
-            each(swap_send.at[0], swap2.at[4], 0, device)
+            each(swap_send.at[0], swap2.at[4], device)
 
     @pl.when(is1)
     def _():
@@ -535,8 +528,15 @@
         swap_send[0] = stat_work[:, 0:128]
         swap3[20 + x] = stat_work[:, 0:128]
 
-    exchange(False)
-    back(False)
+    exchange()
+    back()
+    for head in range(HEADS):
+        att_out[:, DIM * head : DIM * head + DIM] = weighted0[head].T
+    for head in range(HEADS):
+        off = [offsets[head, level] for level in range(3)]
+        spread[head] = jnp.where(
+            iota((TOKENS, 256), 0) == target(iota((1, 256), 1), off), 1.0, 0.0
+        ).astype(BF16)
 
     def below_rows(blocks, head):
         rows = jnp.concatenate(blocks, 1)
@@ -612,7 +612,7 @@
             grad_send3[i] = tile.astype(BF16)
         stack[head3, 160:176] = grad_send3[place]
 
-    grads_back(False)
+    grads_back()
 
     returned1(lambda h: back_stat1.at[h], recv_back1)
     returned23(lambda h: back2.at[h], lambda h: back3.at[h], recv_back)
@@ -667,11 +667,43 @@
         )
         stacked = jnp.concatenate(
             [back_rows1[head], back2[head, 0:32], back3[head, 0:8], jnp.zeros((88, DIM), F32)], 0
-        ).T * share
+        ) * jnp.concatenate([share, jnp.zeros((7, 256), F32)], 0).T[:, 0:1]
         high = stacked.astype(BF16)
         low = (stacked - high.astype(F32)).astype(BF16)
-        attended = shares[head, 0:1] * weighted0[head] + nn(high, sel[head]) + nn(low, sel[head])
-        att_out[:, DIM * head : DIM * head + DIM] = attended.T
+        added = nn(spread[head], jnp.concatenate([high, low], 1))
+        lanes = slice(DIM * head, DIM * head + DIM)
+        att_out[:, lanes] = (
+            att_out[:, lanes] * shares[head].T[:, 0:1] + added[:, 0:DIM] + added[:, DIM : 2 * DIM]
+        )
+
+    for sems, refs in ((send_in, (pack1, pack2, in3)), (send_stat, (tiles1, tiles2, tiles3))):
+        for level, (here, count) in enumerate(((is1, 2), (is2, 2), (is3, 8))):
+            @pl.when(here)
+            def _(ref=refs[level], sem=sems.at[level], count=count):
+                arrived(ref.at[pl.ds(0, count - 1)], sem)
+
+            @pl.when(jnp.logical_not(here))
+            def _(ref=refs[level], sem=sems.at[level], count=count):
+                arrived(ref.at[pl.ds(0, count)], sem)
+
+    @pl.when(is1)
+    def _():
+        arrived(swap3.at[pl.ds(0, 5)], send_swap.at[0])
+        arrived(stat_send.at[pl.ds(0, 3)], send_back1.at[0])
+        arrived(weighted_work.at[pl.ds(0, 384)], send_rows1.at[0])
+        arrived(grad_work.at[pl.ds(0, 384)], send_grad1.at[0])
+
+    @pl.when(is2)
+    def _():
+        arrived(swap3.at[pl.ds(0, 8)], send_swap.at[0])
+        arrived(send2.at[pl.ds(0, 15)], send_back.at[0])
+        arrived(grad_work.at[pl.ds(0, 480)], send_grad.at[0])
+
+    @pl.when(is3)
+    def _():
+        arrived(swap3.at[pl.ds(0, 8)], send_swap.at[0])
+        arrived(send3.at[pl.ds(0, 15)], send_back.at[0])
+        arrived(grad_send3.at[pl.ds(0, 15)], send_grad.at[0])
 
     stack_out[:, 176:256] = jnp.zeros((2, 80, 3 * DIM), BF16)
     returned1(lambda h: stack.at[h, pl.ds(0, 128)], recv_grad1)
@@ -679,14 +711,6 @@
         lambda h: stack.at[h, pl.ds(128, 32)], lambda h: stack.at[h, pl.ds(160, 16)], recv_grad
     )
     stack_out[:, 0:176] = stack[...]
-
-    for device, copy in pending:
-        @pl.when(device != me)
-        def _(copy=copy):
-            copy.wait_send()
-    exchange(True)
-    back(True)
-    grads_back(True)
 
 
 def finish(att, dq, dk, dv, spread, stack, att_out, dq_out, dk_out, dv_out, full, sems):
@@ -731,6 +755,8 @@
         scratch_shapes=[
             pltpu.SMEM((HEADS, 3), jnp.int32),
             held, held, held, held,
+            pltpu.VMEM((2, 4, 48, 256), BF16),
+            pltpu.VMEM((2, 16, 256), F32),
             pltpu.VMEM((2, 256, TOKENS), BF16),
             pltpu.VMEM((2, 128, TOKENS), BF16),
             pltpu.VMEM((2, 128, TOKENS), BF16),
@@ -769,13 +795,13 @@
             pltpu.VMEM((5, 8, 128), F32),
             pltpu.VMEM((24, 8, 128), F32),
             dma((5,)),
-            dma((12,)),
-            dma((16,)),
-            dma((4,)),
-            dma((4,)),
-            dma((12,)),
-            dma((16,)),
-            dma((4,)),
+            dma((3,)),
+            dma((1,)),
+            dma((1,)),
+            dma((1,)),
+            dma((3,)),
+            dma((1,)),
+            dma((1,)),
             dma((3,)),
             dma((4,)),
             dma((2,)),
@@ -783,7 +809,7 @@
             dma((3,)),
             dma((4,)),
             dma((2,)),
-            dma((8,)),
+            dma((1,)),
             dma((1,)),
         ],
         compiler_params=pltpu.CompilerParams(

time: 31.8 us -> 30.8 us (0.969); the launches traced: 31.7 us -> 30.2 us
  Pallas kernels: 31 us -> 29.6 us
    pallas_call x1, Pallas kernels: 28.9 us -> 27.5 us  [body(): pl.pallas_call(kernel, out_shape=(out, out, out, out, jax.ShapeDtypeStruc...]
where the time goes in v6:
time: 30.8 us; the launch traced here: 30.2 us
  Pallas kernels  29.6 us (96%)
  between operations  0.64 us (2%)
    pallas_call x1, Pallas kernels, body(): pl.pallas_call(kernel, out_shape=(out, out, out, out, jax.ShapeDtypeStruc...  27.5 us
    pallas_call x1, Pallas kernels, body(): pl.pallas_call(finish, out_shape=(out, out, out, out), in_specs=[vmem] *...  2.13 us

profile of v6, /device:TPU:8, one launch (start us, length us, event | category | flops | bytes accessed | tf_op | source)
XLA Modules:
  0.0 30.2 jit_solution(17670900618404747080)
XLA Ops:
  0.6 27.5 %shard_map.84 = (f32[1024,256]{1,0:T(8,128)S(1)}, f32[1024,256]{1,0:T(8,128)S(1)}, f32[1024,256]{1,0:T(8,128)S(1)}, f32[1024,256]{1,0:T(8,128)S(1)}, bf16[2,1024...) custom-call(s32[2,3]{1,0:T(2,128)} %bitcast.1, bf16[1024,256]{1,0:T(8,128)(2,1)} %query_hbm.1, ...), custom_call_target="tpu_custom_call" | custom-call | tf_op jit(solution)/shard_map/pallas_call | solution.py:746
  28.1 2.1 %shard_map.85 = (f32[1024,256]{1,0:T(8,128)}, f32[1024,256]{1,0:T(8,128)}, f32[1024,256]{1,0:T(8,128)}, f32[1024,256]{1,0:T(8,128)}) custom-call(f32[1024,256]{1,0:T(8,128)S(1)} %get-tuple-element.10.att, f32[1024,256]{1,0:T(8,128)S(1)} %get-tuple-element.11.dq, f32[1024,256]{1,0:T(8,128)S(1)} %get-tuple-element.12.dk, ...), custom_call_target="tpu_custom_call" | custom-call | tf_op jit(solution)/shard_map/pallas_call | solution.py:819

commit v7 on v6

--- a/solution.py
+++ b/solution.py
@@ -179,7 +179,7 @@
     mine1 = pl.ds(pl.multiple_of(128 * y, 128), 128)
     mine2 = pl.ds(pl.multiple_of(32 * place, 32), 32)
     for head in range(HEADS):
-        send(pack1.at[head], work.at[mine1], send_in.at[0], recv_in.at[0],
+        send(pack1.at[head, :, 0:384], work.at[mine1, 0:384], send_in.at[0], recv_in.at[0],
              group + worker1[head])
     for block in range(4):
         for head in range(HEADS):
@@ -189,6 +189,10 @@
         send(pack2.at[head], work.at[mine2], send_in.at[1], recv_in.at[1],
              plane + worker2[head])
 
+    for head in range(HEADS):
+        send(pack1.at[head, :, 384:512], work.at[mine1, 384:512], send_in.at[3], recv_in.at[3],
+             group + worker1[head])
+
     @pl.when(is1)
     def _():
         work[mine1] = pack1[head12]
@@ -202,17 +206,15 @@
         in3[me] = pack3[head3]
 
     def unit_refs(unit):
-        head = lax.div(unit, 2)
-        segment = lax.rem(unit, 2)
-        return head, segment, pl.ds(pl.multiple_of(DIM * head, DIM), DIM)
-
-    def forward0(unit, carry):
+        head, segment = unit // 2, unit % 2
+        return head, segment, pl.ds(DIM * head, DIM)
+
+    def forward0(unit):
         head, segment, lanes = unit_refs(unit)
-        rows = pl.ds(pl.multiple_of(KEYS * segment, KEYS), KEYS)
+        rows = pl.ds(KEYS * segment, KEYS)
         key, value = keys[rows, lanes], values[rows, lanes]
         for chunk in range(2):
-            start = pl.multiple_of(KEYS * segment + 256 * chunk, 256)
-            part = pl.ds(start, 256)
+            part = pl.ds(KEYS * segment + 256 * chunk, 256)
             scores = nt(key, query[part, lanes]) * FACTOR
             row_max = jnp.max(scores, 0, keepdims=True)
             powers = jnp.exp(scores - row_max)
@@ -224,10 +226,10 @@
             stat0[head, 0:1, part] = row_max
             stat0[head, 1:2, part] = jnp.sum(powers, 0, keepdims=True)
             stat0[head, 2:3, part] = jnp.sum(weights.astype(F32) * products, 0, keepdims=True)
-        return carry
 
     stat0[...] = jnp.zeros_like(stat0)
-    lax.fori_loop(0, 4, forward0, 0)
+    for unit in range(4):
+        forward0(unit)
     bases = (0, 32 * y, 8 * place)
 
     def target(index, off):
@@ -310,26 +312,28 @@
     def of_level(rows, member):
         return jnp.where(member, rows[0:1], -jnp.inf), rows[1:2], rows[2:3]
 
-    def whole_forward():
+    def whole_powers():
         for chunk in range(2):
             part = slice(256 * chunk, 256 * chunk + 256)
             scores = nt(work[:, 0:128], work[part, 256:384]) * FACTOR
             row_max = jnp.max(scores, 0, keepdims=True)
             powers = jnp.exp(scores - row_max)
-            weights = powers.astype(BF16)
+            power_work[:, part] = powers
+            stat_work[0:1, part] = row_max
+            stat_work[1:2, part] = jnp.sum(powers, 0, keepdims=True)
+
+    def whole_products():
+        for chunk in range(2):
+            part = slice(256 * chunk, 256 * chunk + 256)
             products = nt(work[:, 128:256], work[part, 384:512])
-            power_work[:, part] = powers
             product_work[:, part] = products
-            stat_work[:, part] = jnp.concatenate(
-                [
-                    row_max,
-                    jnp.sum(powers, 0, keepdims=True),
-                    jnp.sum(weights.astype(F32) * products, 0, keepdims=True),
-                    jnp.zeros((5, 256), F32),
-                ],
-                0,
-            )
-            weighted_work[part] = tn(weights, work[:, 128:256])
+            weights = power_work[:, part].astype(BF16)
+            stat_work[2:3, part] = jnp.sum(weights.astype(F32) * products, 0, keepdims=True)
+
+    def whole_weighted():
+        for chunk in range(2):
+            part = slice(256 * chunk, 256 * chunk + 256)
+            weighted_work[part] = tn(power_work[:, part].astype(BF16), work[:, 128:256])
 
     def whole_backward(log_row, delta_row):
         grad_k = jnp.zeros((KEYS, DIM), F32)
@@ -365,7 +369,6 @@
             0,
         )
         stat_work[:, 0:128] = stats
-        return tn(weights, work[:, 128:256]), stats
 
     def block_backward(log_all, delta_all, log_own, delta_own):
         k_all, q_all, d_all = work[:, 0:128], work[:, 256:384], work[:, 384:512]
@@ -448,7 +451,7 @@
 
     @pl.when(is1)
     def _():
-        arrived(work.at[pl.ds(0, 384)], recv_in.at[0])
+        arrived(work.at[pl.ds(0, 384), pl.ds(0, 384)], recv_in.at[0])
 
     @pl.when(is2)
     def _():
@@ -460,28 +463,20 @@
         both = in3[...].astype(F32)
         work[:, 0:256] = both[:, 0:8].reshape(KEYS, 256).astype(BF16)
         work[:, 256:512] = both[:, 8:16].reshape(KEYS, 256).astype(BF16)
-        weighted, stats = block_forward()
-        for i in range(16):
-            send3[i] = jnp.concatenate([weighted[8 * i : 8 * i + 8], stats], 0)
-        back3[head3] = send3[place]
+        block_forward()
 
     @pl.when(is1 | is2)
     def _():
-        whole_forward()
+        stat_work[...] = jnp.zeros_like(stat_work)
+        whole_powers()
+
+        @pl.when(is1)
+        def _():
+            arrived(work.at[pl.ds(0, 384), pl.ds(384, 128)], recv_in.at[3])
+
+        whole_products()
         for i in range(4):
             stat_send[i] = stat_work[:, 128 * i : 128 * i + 128]
-
-        @pl.when(is2)
-        def _():
-            for i in range(16):
-                send2[i, 0:32] = weighted_work[32 * i : 32 * i + 32]
-                send2[i, 32:40] = stat_send[i // 4]
-            back2[head12] = send2[place]
-
-        @pl.when(is1)
-        def _():
-            back_stat1[head12] = stat_send[y]
-            back_rows1[head12] = weighted_work[mine1]
 
     def exchange():
         def each(src, dst, device):
@@ -529,6 +524,30 @@
         swap3[20 + x] = stat_work[:, 0:128]
 
     exchange()
+
+    @pl.when(is1 | is2)
+    def _():
+        whole_weighted()
+
+        @pl.when(is2)
+        def _():
+            for i in range(16):
+                send2[i, 0:32] = weighted_work[32 * i : 32 * i + 32]
+                send2[i, 32:40] = stat_send[i // 4]
+            back2[head12] = send2[place]
+
+        @pl.when(is1)
+        def _():
+            back_stat1[head12] = stat_send[y]
+            back_rows1[head12] = weighted_work[mine1]
+
+    @pl.when(is3)
+    def _():
+        weighted = tn(power_work[:, 0:128].astype(BF16), work[:, 128:256])
+        for i in range(16):
+            send3[i] = jnp.concatenate([weighted[8 * i : 8 * i + 8], stat_work[:, 0:128]], 0)
+        back3[head3] = send3[place]
+
     back()
     for head in range(HEADS):
         att_out[:, DIM * head : DIM * head + DIM] = weighted0[head].T
@@ -636,14 +655,14 @@
             [jnp.exp(item[0] - peak) * inverse for item in items] + [jnp.zeros((4, TOKENS), F32)], 0
         )
 
-    def backward0(unit, carry):
+    def backward0(unit):
         head, segment, lanes = unit_refs(unit)
-        rows = pl.ds(pl.multiple_of(KEYS * segment, KEYS), KEYS)
+        rows = pl.ds(KEYS * segment, KEYS)
         key = keys[rows, lanes]
         grad_k = jnp.zeros((KEYS, DIM), F32)
         grad_v = jnp.zeros((KEYS, DIM), F32)
         for chunk in range(2):
-            part = pl.ds(pl.multiple_of(KEYS * segment + 256 * chunk, 256), 256)
+            part = pl.ds(KEYS * segment + 256 * chunk, 256)
             rescale = jnp.exp(stat0[head, 0:1, part] - logs[head, 0:1, part])
             probs = powers0[unit, :, 256 * chunk : 256 * chunk + 256] * rescale
             grad_rows = dout[part, lanes]
@@ -654,9 +673,9 @@
             dq_out[part, lanes] = (FACTOR * tn(key, low)).T
         dk_out[rows, lanes] = FACTOR * grad_k
         dv_out[rows, lanes] = grad_v
-        return carry
-
-    lax.fori_loop(0, 4, backward0, 0)
+
+    for unit in range(4):
+        backward0(unit)
 
     returned1(lambda h: back_rows1.at[h], recv_rows1)
     for head in range(HEADS):
@@ -676,8 +695,12 @@
             att_out[:, lanes] * shares[head].T[:, 0:1] + added[:, 0:DIM] + added[:, DIM : 2 * DIM]
         )
 
-    for sems, refs in ((send_in, (pack1, pack2, in3)), (send_stat, (tiles1, tiles2, tiles3))):
-        for level, (here, count) in enumerate(((is1, 2), (is2, 2), (is3, 8))):
+    keys_part, dout_part = pack1.at[:, :, pl.ds(0, 384)], pack1.at[:, :, pl.ds(384, 128)]
+    for sems, refs in (
+        (send_in, (keys_part, pack2, in3, dout_part)),
+        (send_stat, (tiles1, tiles2, tiles3)),
+    ):
+        for level, (here, count) in enumerate(((is1, 2), (is2, 2), (is3, 8), (is1, 2))[: len(refs)]):
             @pl.when(here)
             def _(ref=refs[level], sem=sems.at[level], count=count):
                 arrived(ref.at[pl.ds(0, count - 1)], sem)
@@ -795,14 +818,14 @@
             pltpu.VMEM((5, 8, 128), F32),
             pltpu.VMEM((24, 8, 128), F32),
             dma((5,)),
-            dma((3,)),
+            dma((4,)),
             dma((1,)),
             dma((1,)),
             dma((1,)),
             dma((3,)),
             dma((1,)),
             dma((1,)),
-            dma((3,)),
+            dma((4,)),
             dma((4,)),
             dma((2,)),
             dma((2,)),

time: 30.8 us -> 30.7 us (level)
  no operation moved by 1% of the time
where the time goes in v7:
time: 30.7 us; the launch traced here: 30.1 us
  Pallas kernels  29.3 us (95%)
  between operations  0.8 us (3%)
    pallas_call x1, Pallas kernels, body(): pl.pallas_call(kernel, out_shape=(out, out, out, out, jax.ShapeDtypeStruc...  27.2 us
    pallas_call x1, Pallas kernels, body(): pl.pallas_call(finish, out_shape=(out, out, out, out), in_specs=[vmem] *...  2.13 us

profile of v7, /device:TPU:8, one launch (start us, length us, event | category | flops | bytes accessed | tf_op | source)
XLA Modules:
  0.0 30.1 jit_solution(15732261419533274929)
XLA Ops:
  0.6 27.2 %shard_map.84 = (f32[1024,256]{1,0:T(8,128)S(1)}, f32[1024,256]{1,0:T(8,128)S(1)}, f32[1024,256]{1,0:T(8,128)S(1)}, f32[1024,256]{1,0:T(8,128)S(1)}, bf16[2,1024...) custom-call(s32[2,3]{1,0:T(2,128)} %bitcast.1, bf16[1024,256]{1,0:T(8,128)(2,1)} %query_hbm.1, ...), custom_call_target="tpu_custom_call" | custom-call | tf_op jit(solution)/shard_map/pallas_call | solution.py:769
  27.8 2.1 %shard_map.85 = (f32[1024,256]{1,0:T(8,128)}, f32[1024,256]{1,0:T(8,128)}, f32[1024,256]{1,0:T(8,128)}, f32[1024,256]{1,0:T(8,128)}) custom-call(f32[1024,256]{1,0:T(8,128)S(1)} %get-tuple-element.10.att, f32[1024,256]{1,0:T(8,128)S(1)} %get-tuple-element.11.dq, f32[1024,256]{1,0:T(8,128)S(1)} %get-tuple-element.12.dk, ...), custom_call_target="tpu_custom_call" | custom-call | tf_op jit(solution)/shard_map/pallas_call | solution.py:842
